TPU v7x, 256 devices: a whole 4x4x8 slice. The times are simulated.
256 devices in a mesh: slab: 64 (over y, z, core), tile: 4 (over x).
Axes of the slice: x: 4, y: 4, z: 8, core: 2. Of those that a mesh axis runs over, the one named last changes fastest.
Arguments:
- positions: bfloat16 [16384, 3, 128], P('slab'), may hold values from 0 to 2
- charges: bfloat16 [16384, 128], P('slab'), may hold values from -0.1796875 to 0.1796875
- leaf_counts: int32 [16384], P('slab'), may hold values from 16 to 128
- multipoles: bfloat16 [16384, 128], P('slab'), may hold values from -6 to 6
- m2l_ops: bfloat16 [316, 128, 128], P('tile'), may hold values from -0.0390625 to 0.0390625
- leaf_send: int32 [576, 256], P('slab', 'tile'), may hold values from -1 to 255, as said below
- pair_slots: int32 [16384, 28], P('slab', 'tile'), may hold values from -1 to 575, as said below
- far_send: int32 [576, 768], P('slab', 'tile'), may hold values from -1 to 255, as said below
- far_slots: int32 [16384, 316], P('slab', 'tile'), may hold values from -1 to 1727, as said below
Outputs:
- near_potential: float32 [16384, 128], P(('slab', 'tile'))
- local_expansion: float32 [16384, 128], P(('slab', 'tile'))
Inputs may be any that keep to these rules, and one draw needn't show every extreme that they name: `leaf_send`: row s * 9 + k, columns t * 64 to t * 64 + 63, lists the local leaves that tile t of slab s sends to tile t of slab s + k - 4: when that slab exists, one to 64 live slots first, then -1; rows for slabs outside the mesh are all -1; every receiving device gets 64 leaves from at least one slab. `pair_slots`: columns t * 7 onward belong to tile t and name a received slot k * 64 + c that is live in leaf_send for sending slab r - k + 4, or -1 for an empty column; every live received slot is named by some column. `far_send`: as leaf_send, for multipoles with 192 slots a route and tile. `far_slots`: columns t * 79 onward belong to tile t and name a received multipole slot k * 192 + c that is live in far_send, or -1; every live received slot is named.
All inputs are finite; a program needn't handle non-finite values.
Results may differ from a plain program's by a relative error of at most 0.00035.
Values may be sent and summed in bfloat16 or wider, within the bound.
No kernel may reach another device: no remote copies, remote signals or barrier semaphores. Data moves between devices by JAX's collectives and lax.ppermute only.
A program may use at most 64 MiB of HBM per device.

v0:
```python
import jax
import jax.numpy as jnp
from jax import lax
from jax.sharding import PartitionSpec as P


def shifted(value, axis, steps):
    count = lax.axis_size(axis)
    initial, last = (max(0, -steps), min(count, count - steps))
    return lax.ppermute(value, axis, [(source, source + steps) for source in range(initial, last)])


def pair_block(operands):
    target_raw, source_raw = operands
    target_pos = target_raw.astype(jnp.float32)
    source_pos = source_raw[:, :, 0:3, :].astype(jnp.float32)
    source_q = source_raw[:, :, 3, :].astype(jnp.float32)
    distance = jnp.zeros(
        (source_pos.shape[0], source_pos.shape[1], target_pos.shape[2], source_pos.shape[3]),
        jnp.float32,
    )
    for coord in range(3):
        delta = target_pos[:, None, coord, :, None] - source_pos[:, :, coord, None, :]
        distance = distance + delta * delta
    inverse = lax.rsqrt(distance + 0.09)
    return jnp.sum(inverse * source_q[:, :, None, :], axis=(1, 3))


def near_field(targets, sources):
    leaf_total = targets.shape[0]
    block_leaves = min(16, leaf_total)
    block_count = leaf_total // block_leaves
    result = lax.map(
        pair_block,
        (
            targets.reshape((block_count, block_leaves) + targets.shape[1:]),
            sources.reshape((block_count, block_leaves) + sources.shape[1:]),
        ),
    )
    return result.reshape(leaf_total, targets.shape[2])


def per_device(
    positions, charges, leaf_counts, multipoles, m2l_ops, leaf_send, pair_slots, far_send, far_slots
):
    slab_leaves, lane_count = charges.shape
    coef_count = multipoles.shape[1]
    op_count = m2l_ops.shape[0]
    peer_count = leaf_send.shape[0]
    reach = (peer_count - 1) // 2
    lane_ids = jnp.arange(lane_count, dtype=jnp.int32)
    charge_mask = lane_ids[None, :] < leaf_counts[:, None]
    masked_q = jnp.where(charge_mask, charges, jnp.zeros_like(charges))
    leaf_rows = jnp.concatenate([positions, masked_q[:, None, :]], axis=1).reshape(
        slab_leaves, 4 * lane_count
    )
    outgoing_leaves = leaf_rows[jnp.maximum(leaf_send, 0)]
    outgoing_multi = multipoles[jnp.maximum(far_send, 0)]
    leaf_list = []
    multi_list = []
    for offset in range(peer_count):
        distance_by = offset - reach
        if distance_by == 0:
            leaf_list.append(outgoing_leaves[offset])
            multi_list.append(outgoing_multi[offset])
        else:
            moved_leaves, moved_multi = shifted(
                (outgoing_leaves[offset], outgoing_multi[offset]), "slab", distance_by
            )
            leaf_list.append(moved_leaves)
            multi_list.append(moved_multi)
    got_leaves = jnp.stack(leaf_list, axis=0)
    got_multi = jnp.stack(multi_list, axis=0)
    near_flat = got_leaves.reshape(-1, 4 * lane_count)
    near_slots = near_flat.shape[0]
    near_flat = jnp.concatenate(
        [near_flat, jnp.zeros((1, 4 * lane_count), near_flat.dtype)], axis=0
    )
    near_index = jnp.where(pair_slots >= 0, pair_slots, near_slots)
    sources = near_flat[near_index].reshape(slab_leaves, pair_slots.shape[1], 4, lane_count)
    near = near_field(positions, sources)
    near = jnp.where(charge_mask, near, jnp.zeros((), jnp.float32))
    far_flat = got_multi.reshape(-1, coef_count)
    far_count = far_flat.shape[0]
    far_flat = jnp.concatenate([far_flat, jnp.zeros((1, coef_count), far_flat.dtype)], axis=0)
    far_index = jnp.where(far_slots >= 0, far_slots, far_count)
    regrouped = far_flat[far_index.reshape(-1)].reshape(slab_leaves, op_count * coef_count)
    local = jnp.dot(
        regrouped,
        m2l_ops.reshape(op_count * coef_count, coef_count),
        preferred_element_type=jnp.float32,
    )
    near_part, local_part = (
        lax.psum_scatter(near, "tile", scatter_dimension=0, tiled=True),
        lax.psum_scatter(local, "tile", scatter_dimension=0, tiled=True),
    )
    return (near_part, local_part)


def solution(mesh):
    return jax.shard_map(
        per_device,
        mesh=mesh,
        in_specs=(
            P("slab", None, None),
            P("slab", None),
            P("slab"),
            P("slab", None),
            P("tile", None, None),
            P("slab", "tile"),
            P("slab", "tile"),
            P("slab", "tile"),
            P("slab", "tile"),
        ),
        out_specs=(P(("slab", "tile"), None), P(("slab", "tile"), None)),
        check_vma=False,
    )
```

profile of v0, /device:TPU:6, one launch (start us, length us, event | category | flops | bytes accessed | tf_op | source)
XLA Modules:
  0.0 263.0 jit_solution(6698035583808009595)
XLA Ops:
  9.3 4.2 %gather_fusion.2 = bf16[1728,128]{1,0:T(8,128)(2,1)S(1)} fusion(bf16[256,128]{1,0:T(8,128)(2,1)} %param.14, s32[2048]{0:T(1024)S(1)} %get-tuple-element.67), kind=kCustom, calls=%fused_computation.2 | custom fusion | bytes 891648 | tf_op jit(solution)/shard_map/gather | solution.py:58
  14.3 1.3 collective-permute-start.8
  15.6 1.3 collective-permute-start.9
  16.9 1.3 collective-permute-start.10
  18.2 1.3 collective-permute-start.11
  19.5 3.6 %collective-permute-start.12 = (bf16[192,128]{1,0:T(8,128)(2,1)}, bf16[192,128]{1,0:T(8,128)(2,1)}, u32[]{:S(2)}, u32[]{:S(2)}) collective-permute-start(bf16[192,128]{1,0:T(8,128)(2,1)} %get-tuple-element.62), channel_id=1, source_target_pairs={{0,4},{4,8},{8,12},{12,16},{16,20},{20,24},{24,28},{28,32},{32,36}... | collective-permute-start | bytes 147464 | tf_op jit(solution)/shard_map/ppermute | solution.py:10
  24.1 3.2 %gather_fusion = bf16[576,512]{1,0:T(8,128)(2,1)} fusion(bf16[256,512]{1,0:T(8,128)(2,1)S(1)} %copy_bitcast_fusion.1, s32[1024]{0:T(1024)S(1)} %pad_clamp_fusion.3), kind=kCustom, calls=%fused_computation | custom fusion | bytes 1181952 | tf_op jit(solution)/shard_map/gather | solution.py:57
  27.4 1.8 fusion.6
  29.2 4.2 %collective-permute-start.13 = (bf16[192,128]{1,0:T(8,128)(2,1)S(1)}, bf16[192,128]{1,0:T(8,128)(2,1)S(1)}, u32[]{:S(2)}, u32[]{:S(2)}) collective-permute-start(bf16[192,128]{1,0:T(8,128)(2,1)S(1)} %copy-done.9), channel_id=1, source_target_pairs={{0,8},{4,12},{8,16},{12,20},{16,24},{20,28},{24,32},{28,36},{32,40... | collective-permute-start | bytes 147464 | tf_op jit(solution)/shard_map/ppermute | solution.py:10
  34.3 5.7 %collective-permute-start.14 = (bf16[192,128]{1,0:T(8,128)(2,1)S(1)}, bf16[192,128]{1,0:T(8,128)(2,1)S(1)}, u32[]{:S(2)}, u32[]{:S(2)}) collective-permute-start(bf16[192,128]{1,0:T(8,128)(2,1)S(1)} %copy-done.8), channel_id=1, source_target_pairs={{0,12},{4,16},{8,20},{12,24},{16,28},{20,32},{24,36},{28,40},{32,4... | collective-permute-start | bytes 147464 | tf_op jit(solution)/shard_map/ppermute | solution.py:10
  40.8 6.4 %collective-permute-start.15 = (bf16[192,128]{1,0:T(8,128)(2,1)S(1)}, bf16[192,128]{1,0:T(8,128)(2,1)S(1)}, u32[]{:S(2)}, u32[]{:S(2)}) collective-permute-start(bf16[192,128]{1,0:T(8,128)(2,1)S(1)} %copy-done.7), channel_id=1, source_target_pairs={{0,16},{4,20},{8,24},{12,28},{16,32},{20,36},{24,40},{28,44},{32,4... | collective-permute-start | bytes 147464 | tf_op jit(solution)/shard_map/ppermute | solution.py:10
  48.0 1.3 collective-permute-start
  50.9 1.3 collective-permute-start.1
  53.0 1.3 collective-permute-start.2
  54.4 1.3 collective-permute-start.3
  55.7 3.7 %collective-permute-start.4 = (bf16[64,512]{1,0:T(8,128)(2,1)}, bf16[64,512]{1,0:T(8,128)(2,1)}, u32[]{:S(2)}, u32[]{:S(2)}) collective-permute-start(bf16[64,512]{1,0:T(8,128)(2,1)} %get-tuple-element.54), channel_id=1, source_target_pairs={{0,4},{4,8},{8,12},{12,16},{16,20},{20,24},{24,28},{28,32},{32,36}... | collective-permute-start | bytes 196616 | tf_op jit(solution)/shard_map/ppermute | solution.py:10
  59.4 41.2 %gather_fusion.3 = bf16[20224,128]{1,0:T(8,128)(2,1)} fusion(bf16[1729,128]{1,0:T(8,128)(2,1)S(1)} %concatenate.11, s32[20480]{0:T(1024)S(1)} %pad_clamp_fusion), kind=kCustom, calls=%fused_computation.3 | custom fusion | bytes 10435584 | tf_op jit(solution)/shard_map/gather | solution.py:87
  100.7 9.6 %reshape.68 = bf16[256,10112]{1,0:T(8,128)(2,1)} reshape(bf16[20224,128]{1,0:T(8,128)(2,1)} %gather_fusion.3) | data formatting | bytes 10354688 | tf_op jit(solution)/shard_map/reshape | solution.py:87
  110.3 4.7 %fusion.8 = f32[256,128]{1,0:T(8,128)} fusion(bf16[256,10112]{1,0:T(8,128)(2,1)} %reshape.68, bf16[10112,128]{1,0:T(8,128)(2,1)S(1)} %bitcast.94), kind=kOutput, calls=%fused_computation.57 | convolution fusion | flops 662700032 | bytes 7897088 | tf_op jit(solution)/shard_map/dot_general | solution.py:88
  115.0 4.2 %collective-permute-start.5 = (bf16[64,512]{1,0:T(8,128)(2,1)S(1)}, bf16[64,512]{1,0:T(8,128)(2,1)S(1)}, u32[]{:S(2)}, u32[]{:S(2)}) collective-permute-start(bf16[64,512]{1,0:T(8,128)(2,1)S(1)} %copy-done.5), channel_id=1, source_target_pairs={{0,8},{4,12},{8,16},{12,20},{16,24},{20,28},{24,32},{28,36},{32,40... | collective-permute-start | bytes 196616 | tf_op jit(solution)/shard_map/ppermute | solution.py:10
  120.1 7.2 %collective-permute-start.6 = (bf16[64,512]{1,0:T(8,128)(2,1)S(1)}, bf16[64,512]{1,0:T(8,128)(2,1)S(1)}, u32[]{:S(2)}, u32[]{:S(2)}) collective-permute-start(bf16[64,512]{1,0:T(8,128)(2,1)S(1)} %copy-done.4), channel_id=1, source_target_pairs={{0,12},{4,16},{8,20},{12,24},{16,28},{20,32},{24,36},{28,40},{32,4... | collective-permute-start | bytes 196616 | tf_op jit(solution)/shard_map/ppermute | solution.py:10
  128.1 6.3 %collective-permute-start.7 = (bf16[64,512]{1,0:T(8,128)(2,1)S(1)}, bf16[64,512]{1,0:T(8,128)(2,1)S(1)}, u32[]{:S(2)}, u32[]{:S(2)}) collective-permute-start(bf16[64,512]{1,0:T(8,128)(2,1)S(1)} %get-tuple-element.51), channel_id=1, source_target_pairs={{0,16},{4,20},{8,24},{12,28},{16,32},{20,36},{24,40},{28,44},{32,4... | collective-permute-start | bytes 196616 | tf_op jit(solution)/shard_map/ppermute | solution.py:10
  137.9 6.2 %gather_fusion.1 = bf16[1792,512]{1,0:T(8,128)(2,1)} fusion(bf16[577,512]{1,0:T(8,128)(2,1)S(1)} %concatenate.10, s32[2048]{0:T(1024)S(1)} %get-tuple-element.68), kind=kCustom, calls=%fused_computation.1 | custom fusion | bytes 3677184 | tf_op jit(solution)/shard_map/gather | solution.py:80
  144.1 4.2 %reshape_reshape.3 = bf16[16,16,7,4,128]{4,3,2,1,0:T(4,128)(2,1)} reshape(bf16[1792,512]{1,0:T(8,128)(2,1)} %gather_fusion.1) | data formatting | bytes 3670016 | tf_op jit(solution)/shard_map/reshape;reshape | solution.py:37
  148.3 82.4 %while.10 = (s32[]{:T(128)}, f32[16,16,128]{2,1,0:T(8,128)S(1)}, bf16[16,16,3,128]{3,1,0,2:T(8,128)(2,1)S(1)}, bf16[16,16,7,4,128]{4,3,2,1,0:T(4,128)(2,1)}, s32[]{:T(128)}) while((s32[]{:T(128)}, f32[16,16,128]{2,1,0:T(8,128)S(1)}, bf16[16,16,3,128]{3,1,0,2:T(8,128)(2,1)S(1)}, bf16[16,16,7,4,128]{4,3,2,1,0:T(4,128)(2,1)}, s32[]{:T(128)}) %tuple.55), condition=%wide.region_2.3_spmd, body=%wide.region_0.2_spmd.sunk | while | flops 20246528 | bytes 1970249 | solution.py:33
  149.5 3.9 %multiply_reduce_fusion.2 = f32[16,128]{1,0:T(8,128)S(1)} fusion(f32[16,7,128]{2,1,0:T(8,128)S(1)} %copy.51, f32[16,7,128]{2,1,0:T(8,128)S(1)} %copy.52, f32[16,128]{1,0:T(8,128)S(1)} %get-tuple-element.101, f32[16,7,128]{2,1,0:T(8,128)S(1)} %copy.53, f32[16,128]{1,0:T(8,128)S(1)} %get-tuple-element.103, f32[16,7,128]{2,1,0:T(8,128)S(1)} %copy.54, ...), kind=kLoop, calls=%fused_computation.4.clone.1 | loop fusion | flops 20183040 | bytes 262144 | tf_op jit(solution)/shard_map/while/body/eval_jaxpr/reduce_sum | solution.py:26
  153.4 0.9 constant_dynamic-slice_fusion.2
  154.6 3.9 %multiply_reduce_fusion.2 = f32[16,128]{1,0:T(8,128)S(1)} fusion(f32[16,7,128]{2,1,0:T(8,128)S(1)} %copy.51, f32[16,7,128]{2,1,0:T(8,128)S(1)} %copy.52, f32[16,128]{1,0:T(8,128)S(1)} %get-tuple-element.101, f32[16,7,128]{2,1,0:T(8,128)S(1)} %copy.53, f32[16,128]{1,0:T(8,128)S(1)} %get-tuple-element.103, f32[16,7,128]{2,1,0:T(8,128)S(1)} %copy.54, ...), kind=kLoop, calls=%fused_computation.4.clone.1 | loop fusion | flops 20183040 | bytes 262144 | tf_op jit(solution)/shard_map/while/body/eval_jaxpr/reduce_sum | solution.py:26
  158.6 0.9 constant_dynamic-slice_fusion.2
  159.8 3.9 %multiply_reduce_fusion.2 = f32[16,128]{1,0:T(8,128)S(1)} fusion(f32[16,7,128]{2,1,0:T(8,128)S(1)} %copy.51, f32[16,7,128]{2,1,0:T(8,128)S(1)} %copy.52, f32[16,128]{1,0:T(8,128)S(1)} %get-tuple-element.101, f32[16,7,128]{2,1,0:T(8,128)S(1)} %copy.53, f32[16,128]{1,0:T(8,128)S(1)} %get-tuple-element.103, f32[16,7,128]{2,1,0:T(8,128)S(1)} %copy.54, ...), kind=kLoop, calls=%fused_computation.4.clone.1 | loop fusion | flops 20183040 | bytes 262144 | tf_op jit(solution)/shard_map/while/body/eval_jaxpr/reduce_sum | solution.py:26
  163.8 0.9 constant_dynamic-slice_fusion.2
  164.9 3.9 %multiply_reduce_fusion.2 = f32[16,128]{1,0:T(8,128)S(1)} fusion(f32[16,7,128]{2,1,0:T(8,128)S(1)} %copy.51, f32[16,7,128]{2,1,0:T(8,128)S(1)} %copy.52, f32[16,128]{1,0:T(8,128)S(1)} %get-tuple-element.101, f32[16,7,128]{2,1,0:T(8,128)S(1)} %copy.53, f32[16,128]{1,0:T(8,128)S(1)} %get-tuple-element.103, f32[16,7,128]{2,1,0:T(8,128)S(1)} %copy.54, ...), kind=kLoop, calls=%fused_computation.4.clone.1 | loop fusion | flops 20183040 | bytes 262144 | tf_op jit(solution)/shard_map/while/body/eval_jaxpr/reduce_sum | solution.py:26
  168.9 0.9 constant_dynamic-slice_fusion.2
  170.1 3.9 %multiply_reduce_fusion.2 = f32[16,128]{1,0:T(8,128)S(1)} fusion(f32[16,7,128]{2,1,0:T(8,128)S(1)} %copy.51, f32[16,7,128]{2,1,0:T(8,128)S(1)} %copy.52, f32[16,128]{1,0:T(8,128)S(1)} %get-tuple-element.101, f32[16,7,128]{2,1,0:T(8,128)S(1)} %copy.53, f32[16,128]{1,0:T(8,128)S(1)} %get-tuple-element.103, f32[16,7,128]{2,1,0:T(8,128)S(1)} %copy.54, ...), kind=kLoop, calls=%fused_computation.4.clone.1 | loop fusion | flops 20183040 | bytes 262144 | tf_op jit(solution)/shard_map/while/body/eval_jaxpr/reduce_sum | solution.py:26
  175.2 3.9 %multiply_reduce_fusion.2 = f32[16,128]{1,0:T(8,128)S(1)} fusion(f32[16,7,128]{2,1,0:T(8,128)S(1)} %copy.51, f32[16,7,128]{2,1,0:T(8,128)S(1)} %copy.52, f32[16,128]{1,0:T(8,128)S(1)} %get-tuple-element.101, f32[16,7,128]{2,1,0:T(8,128)S(1)} %copy.53, f32[16,128]{1,0:T(8,128)S(1)} %get-tuple-element.103, f32[16,7,128]{2,1,0:T(8,128)S(1)} %copy.54, ...), kind=kLoop, calls=%fused_computation.4.clone.1 | loop fusion | flops 20183040 | bytes 262144 | tf_op jit(solution)/shard_map/while/body/eval_jaxpr/reduce_sum | solution.py:26
  179.2 0.9 constant_dynamic-slice_fusion.2
  180.4 3.9 %multiply_reduce_fusion.2 = f32[16,128]{1,0:T(8,128)S(1)} fusion(f32[16,7,128]{2,1,0:T(8,128)S(1)} %copy.51, f32[16,7,128]{2,1,0:T(8,128)S(1)} %copy.52, f32[16,128]{1,0:T(8,128)S(1)} %get-tuple-element.101, f32[16,7,128]{2,1,0:T(8,128)S(1)} %copy.53, f32[16,128]{1,0:T(8,128)S(1)} %get-tuple-element.103, f32[16,7,128]{2,1,0:T(8,128)S(1)} %copy.54, ...), kind=kLoop, calls=%fused_computation.4.clone.1 | loop fusion | flops 20183040 | bytes 262144 | tf_op jit(solution)/shard_map/while/body/eval_jaxpr/reduce_sum | solution.py:26
  185.6 3.9 %multiply_reduce_fusion.2 = f32[16,128]{1,0:T(8,128)S(1)} fusion(f32[16,7,128]{2,1,0:T(8,128)S(1)} %copy.51, f32[16,7,128]{2,1,0:T(8,128)S(1)} %copy.52, f32[16,128]{1,0:T(8,128)S(1)} %get-tuple-element.101, f32[16,7,128]{2,1,0:T(8,128)S(1)} %copy.53, f32[16,128]{1,0:T(8,128)S(1)} %get-tuple-element.103, f32[16,7,128]{2,1,0:T(8,128)S(1)} %copy.54, ...), kind=kLoop, calls=%fused_computation.4.clone.1 | loop fusion | flops 20183040 | bytes 262144 | tf_op jit(solution)/shard_map/while/body/eval_jaxpr/reduce_sum | solution.py:26
  190.7 3.9 %multiply_reduce_fusion.2 = f32[16,128]{1,0:T(8,128)S(1)} fusion(f32[16,7,128]{2,1,0:T(8,128)S(1)} %copy.51, f32[16,7,128]{2,1,0:T(8,128)S(1)} %copy.52, f32[16,128]{1,0:T(8,128)S(1)} %get-tuple-element.101, f32[16,7,128]{2,1,0:T(8,128)S(1)} %copy.53, f32[16,128]{1,0:T(8,128)S(1)} %get-tuple-element.103, f32[16,7,128]{2,1,0:T(8,128)S(1)} %copy.54, ...), kind=kLoop, calls=%fused_computation.4.clone.1 | loop fusion | flops 20183040 | bytes 262144 | tf_op jit(solution)/shard_map/while/body/eval_jaxpr/reduce_sum | solution.py:26
  195.9 3.9 %multiply_reduce_fusion.2 = f32[16,128]{1,0:T(8,128)S(1)} fusion(f32[16,7,128]{2,1,0:T(8,128)S(1)} %copy.51, f32[16,7,128]{2,1,0:T(8,128)S(1)} %copy.52, f32[16,128]{1,0:T(8,128)S(1)} %get-tuple-element.101, f32[16,7,128]{2,1,0:T(8,128)S(1)} %copy.53, f32[16,128]{1,0:T(8,128)S(1)} %get-tuple-element.103, f32[16,7,128]{2,1,0:T(8,128)S(1)} %copy.54, ...), kind=kLoop, calls=%fused_computation.4.clone.1 | loop fusion | flops 20183040 | bytes 262144 | tf_op jit(solution)/shard_map/while/body/eval_jaxpr/reduce_sum | solution.py:26
  201.0 3.9 %multiply_reduce_fusion.2 = f32[16,128]{1,0:T(8,128)S(1)} fusion(f32[16,7,128]{2,1,0:T(8,128)S(1)} %copy.51, f32[16,7,128]{2,1,0:T(8,128)S(1)} %copy.52, f32[16,128]{1,0:T(8,128)S(1)} %get-tuple-element.101, f32[16,7,128]{2,1,0:T(8,128)S(1)} %copy.53, f32[16,128]{1,0:T(8,128)S(1)} %get-tuple-element.103, f32[16,7,128]{2,1,0:T(8,128)S(1)} %copy.54, ...), kind=kLoop, calls=%fused_computation.4.clone.1 | loop fusion | flops 20183040 | bytes 262144 | tf_op jit(solution)/shard_map/while/body/eval_jaxpr/reduce_sum | solution.py:26
  206.2 3.9 %multiply_reduce_fusion.2 = f32[16,128]{1,0:T(8,128)S(1)} fusion(f32[16,7,128]{2,1,0:T(8,128)S(1)} %copy.51, f32[16,7,128]{2,1,0:T(8,128)S(1)} %copy.52, f32[16,128]{1,0:T(8,128)S(1)} %get-tuple-element.101, f32[16,7,128]{2,1,0:T(8,128)S(1)} %copy.53, f32[16,128]{1,0:T(8,128)S(1)} %get-tuple-element.103, f32[16,7,128]{2,1,0:T(8,128)S(1)} %copy.54, ...), kind=kLoop, calls=%fused_computation.4.clone.1 | loop fusion | flops 20183040 | bytes 262144 | tf_op jit(solution)/shard_map/while/body/eval_jaxpr/reduce_sum | solution.py:26
  211.3 3.9 %multiply_reduce_fusion.2 = f32[16,128]{1,0:T(8,128)S(1)} fusion(f32[16,7,128]{2,1,0:T(8,128)S(1)} %copy.51, f32[16,7,128]{2,1,0:T(8,128)S(1)} %copy.52, f32[16,128]{1,0:T(8,128)S(1)} %get-tuple-element.101, f32[16,7,128]{2,1,0:T(8,128)S(1)} %copy.53, f32[16,128]{1,0:T(8,128)S(1)} %get-tuple-element.103, f32[16,7,128]{2,1,0:T(8,128)S(1)} %copy.54, ...), kind=kLoop, calls=%fused_computation.4.clone.1 | loop fusion | flops 20183040 | bytes 262144 | tf_op jit(solution)/shard_map/while/body/eval_jaxpr/reduce_sum | solution.py:26
  215.3 0.9 constant_dynamic-slice_fusion.2
  216.5 3.9 %multiply_reduce_fusion.2 = f32[16,128]{1,0:T(8,128)S(1)} fusion(f32[16,7,128]{2,1,0:T(8,128)S(1)} %copy.51, f32[16,7,128]{2,1,0:T(8,128)S(1)} %copy.52, f32[16,128]{1,0:T(8,128)S(1)} %get-tuple-element.101, f32[16,7,128]{2,1,0:T(8,128)S(1)} %copy.53, f32[16,128]{1,0:T(8,128)S(1)} %get-tuple-element.103, f32[16,7,128]{2,1,0:T(8,128)S(1)} %copy.54, ...), kind=kLoop, calls=%fused_computation.4.clone.1 | loop fusion | flops 20183040 | bytes 262144 | tf_op jit(solution)/shard_map/while/body/eval_jaxpr/reduce_sum | solution.py:26
  221.6 3.9 %multiply_reduce_fusion.2 = f32[16,128]{1,0:T(8,128)S(1)} fusion(f32[16,7,128]{2,1,0:T(8,128)S(1)} %copy.51, f32[16,7,128]{2,1,0:T(8,128)S(1)} %copy.52, f32[16,128]{1,0:T(8,128)S(1)} %get-tuple-element.101, f32[16,7,128]{2,1,0:T(8,128)S(1)} %copy.53, f32[16,128]{1,0:T(8,128)S(1)} %get-tuple-element.103, f32[16,7,128]{2,1,0:T(8,128)S(1)} %copy.54, ...), kind=kLoop, calls=%fused_computation.4.clone.1 | loop fusion | flops 20183040 | bytes 262144 | tf_op jit(solution)/shard_map/while/body/eval_jaxpr/reduce_sum | solution.py:26
  226.8 3.9 %multiply_reduce_fusion.2 = f32[16,128]{1,0:T(8,128)S(1)} fusion(f32[16,7,128]{2,1,0:T(8,128)S(1)} %copy.51, f32[16,7,128]{2,1,0:T(8,128)S(1)} %copy.52, f32[16,128]{1,0:T(8,128)S(1)} %get-tuple-element.101, f32[16,7,128]{2,1,0:T(8,128)S(1)} %copy.53, f32[16,128]{1,0:T(8,128)S(1)} %get-tuple-element.103, f32[16,7,128]{2,1,0:T(8,128)S(1)} %copy.54, ...), kind=kLoop, calls=%fused_computation.4.clone.1 | loop fusion | flops 20183040 | bytes 262144 | tf_op jit(solution)/shard_map/while/body/eval_jaxpr/reduce_sum | solution.py:26
  231.6 24.6 %reduce-scatter.3.cloned.1.call-done = f32[64,128]{1,0:T(8,128)} async-done(((f32[256,128]{1,0:T(8,128)}), f32[64,128]{1,0:T(8,128)}) %reduce-scatter.3.cloned.1.call-update) | async-done | bytes 32784 | tf_op jit(solution)/shard_map/reduce_scatter | solution.py:94
  (270 shorter events, 26.9 us)
Async XLA Ops:
  7.2 103.1 %copy-start = (bf16[79,128,128]{2,1,0:T(8,128)(2,1)S(1)}, bf16[79,128,128]{2,1,0:T(8,128)(2,1)}, u32[]{:S(2)}) copy-start(bf16[79,128,128]{2,1,0:T(8,128)(2,1)} %param.15) | copy-start | bytes 7766020
  7.2 16.0 %copy-start.3 = (s32[256,79]{0,1:T(8,128)S(1)}, s32[256,79]{0,1:T(8,128)}, u32[]{:S(2)}) copy-start(s32[256,79]{0,1:T(8,128)} %param.19) | copy-start | bytes 242692
  7.2 16.6 %copy-start.10 = (s32[9,64]{1,0:T(8,128)S(1)}, s32[9,64]{1,0:T(8,128)}, u32[]{:S(2)}) copy-start(s32[9,64]{1,0:T(8,128)} %param.16) | copy-start | bytes 6916
  7.2 16.7 %copy-start.6 = (bf16[256,128]{1,0:T(8,128)(2,1)S(1)}, bf16[256,128]{1,0:T(8,128)(2,1)}, u32[]{:S(2)}) copy-start(bf16[256,128]{1,0:T(8,128)(2,1)} %param.12) | copy-start | bytes 196612
  7.2 16.7 %copy-start.11 = (s32[256]{0:T(256)S(1)}, s32[256]{0:T(256)}, u32[]{:S(2)}) copy-start(s32[256]{0:T(256)} %param.13) | copy-start | bytes 3076
  7.2 16.8 %copy-start.2 = (bf16[256,3,128]{2,0,1:T(8,128)(2,1)S(1)}, bf16[256,3,128]{2,0,1:T(8,128)(2,1)}, u32[]{:S(2)}) copy-start(bf16[256,3,128]{2,0,1:T(8,128)(2,1)} %param.11) | copy-start | bytes 589828
  7.2 224.3 %reduce-scatter.5.cloned.1.call-start = ((), (), s32[]{:S(2)}) async-start(), calls=%async_computation.3 | async-start | bytes 163840 | tf_op jit(solution)/shard_map/reduce_scatter | solution.py:95
  13.5 10.4 %copy-start.1 = (bf16[1728,128]{1,0:T(8,128)(2,1)}, bf16[1728,128]{1,0:T(8,128)(2,1)S(1)}, u32[]{:S(2)}) copy-start(bf16[1728,128]{1,0:T(8,128)(2,1)S(1)} %gather_fusion.2) | copy-start | bytes 1327108
  14.3 14.9 %collective-permute-start.8 = (bf16[192,128]{1,0:T(8,128)(2,1)}, bf16[192,128]{1,0:T(8,128)(2,1)}, u32[]{:S(2)}, u32[]{:S(2)}) collective-permute-start(bf16[192,128]{1,0:T(8,128)(2,1)} %get-tuple-element.66), channel_id=1, source_target_pairs={{16,0},{20,4},{24,8},{28,12},{32,16},{36,20},{40,24},{44,28},{48,3... | collective-permute-start | bytes 147464 | tf_op jit(solution)/shard_map/ppermute | solution.py:10
  15.6 18.6 %collective-permute-start.9 = (bf16[192,128]{1,0:T(8,128)(2,1)}, bf16[192,128]{1,0:T(8,128)(2,1)}, u32[]{:S(2)}, u32[]{:S(2)}) collective-permute-start(bf16[192,128]{1,0:T(8,128)(2,1)} %get-tuple-element.65), channel_id=1, source_target_pairs={{12,0},{16,4},{20,8},{24,12},{28,16},{32,20},{36,24},{40,28},{44,3... | collective-permute-start | bytes 147464 | tf_op jit(solution)/shard_map/ppermute | solution.py:10
  16.9 23.9 %collective-permute-start.10 = (bf16[192,128]{1,0:T(8,128)(2,1)}, bf16[192,128]{1,0:T(8,128)(2,1)}, u32[]{:S(2)}, u32[]{:S(2)}) collective-permute-start(bf16[192,128]{1,0:T(8,128)(2,1)} %get-tuple-element.64), channel_id=1, source_target_pairs={{8,0},{12,4},{16,8},{20,12},{24,16},{28,20},{32,24},{36,28},{40,32... | collective-permute-start | bytes 147464 | tf_op jit(solution)/shard_map/ppermute | solution.py:10
  18.2 29.8 %collective-permute-start.11 = (bf16[192,128]{1,0:T(8,128)(2,1)}, bf16[192,128]{1,0:T(8,128)(2,1)}, u32[]{:S(2)}, u32[]{:S(2)}) collective-permute-start(bf16[192,128]{1,0:T(8,128)(2,1)} %get-tuple-element.63), channel_id=1, source_target_pairs={{4,0},{8,4},{12,8},{16,12},{20,16},{24,20},{28,24},{32,28},{36,32}... | collective-permute-start | bytes 147464 | tf_op jit(solution)/shard_map/ppermute | solution.py:10
  19.5 31.4 %collective-permute-start.12 = (bf16[192,128]{1,0:T(8,128)(2,1)}, bf16[192,128]{1,0:T(8,128)(2,1)}, u32[]{:S(2)}, u32[]{:S(2)}) collective-permute-start(bf16[192,128]{1,0:T(8,128)(2,1)} %get-tuple-element.62), channel_id=1, source_target_pairs={{0,4},{4,8},{8,12},{12,16},{16,20},{20,24},{24,28},{28,32},{32,36}... | collective-permute-start | bytes 147464 | tf_op jit(solution)/shard_map/ppermute | solution.py:10
  24.1 5.2 %copy-start.9 = (bf16[192,128]{1,0:T(8,128)(2,1)S(1)}, bf16[192,128]{1,0:T(8,128)(2,1)}, u32[]{:S(2)}) copy-start(bf16[192,128]{1,0:T(8,128)(2,1)} %get-tuple-element.61) | copy-start | bytes 147460
  24.1 10.2 %copy-start.8 = (bf16[192,128]{1,0:T(8,128)(2,1)S(1)}, bf16[192,128]{1,0:T(8,128)(2,1)}, u32[]{:S(2)}) copy-start(bf16[192,128]{1,0:T(8,128)(2,1)} %get-tuple-element.60) | copy-start | bytes 147460
  24.1 16.7 %copy-start.7 = (bf16[192,128]{1,0:T(8,128)(2,1)S(1)}, bf16[192,128]{1,0:T(8,128)(2,1)}, u32[]{:S(2)}) copy-start(bf16[192,128]{1,0:T(8,128)(2,1)} %get-tuple-element.59) | copy-start | bytes 147460
  29.2 23.8 %collective-permute-start.13 = (bf16[192,128]{1,0:T(8,128)(2,1)S(1)}, bf16[192,128]{1,0:T(8,128)(2,1)S(1)}, u32[]{:S(2)}, u32[]{:S(2)}) collective-permute-start(bf16[192,128]{1,0:T(8,128)(2,1)S(1)} %copy-done.9), channel_id=1, source_target_pairs={{0,8},{4,12},{8,16},{12,20},{16,24},{20,28},{24,32},{28,36},{32,40... | collective-permute-start | bytes 147464 | tf_op jit(solution)/shard_map/ppermute | solution.py:10
  34.3 20.1 %collective-permute-start.14 = (bf16[192,128]{1,0:T(8,128)(2,1)S(1)}, bf16[192,128]{1,0:T(8,128)(2,1)S(1)}, u32[]{:S(2)}, u32[]{:S(2)}) collective-permute-start(bf16[192,128]{1,0:T(8,128)(2,1)S(1)} %copy-done.8), channel_id=1, source_target_pairs={{0,12},{4,16},{8,20},{12,24},{16,28},{20,32},{24,36},{28,40},{32,4... | collective-permute-start | bytes 147464 | tf_op jit(solution)/shard_map/ppermute | solution.py:10
  40.8 14.9 %collective-permute-start.15 = (bf16[192,128]{1,0:T(8,128)(2,1)S(1)}, bf16[192,128]{1,0:T(8,128)(2,1)S(1)}, u32[]{:S(2)}, u32[]{:S(2)}) collective-permute-start(bf16[192,128]{1,0:T(8,128)(2,1)S(1)} %copy-done.7), channel_id=1, source_target_pairs={{0,16},{4,20},{8,24},{12,28},{16,32},{20,36},{24,40},{28,44},{32,4... | collective-permute-start | bytes 147464 | tf_op jit(solution)/shard_map/ppermute | solution.py:10
  48.0 67.0 %collective-permute-start = (bf16[64,512]{1,0:T(8,128)(2,1)}, bf16[64,512]{1,0:T(8,128)(2,1)}, u32[]{:S(2)}, u32[]{:S(2)}) collective-permute-start(bf16[64,512]{1,0:T(8,128)(2,1)} %get-tuple-element.58), channel_id=1, source_target_pairs={{16,0},{20,4},{24,8},{28,12},{32,16},{36,20},{40,24},{44,28},{48,3... | collective-permute-start | bytes 196616 | tf_op jit(solution)/shard_map/ppermute | solution.py:10
  50.9 69.2 %collective-permute-start.1 = (bf16[64,512]{1,0:T(8,128)(2,1)}, bf16[64,512]{1,0:T(8,128)(2,1)}, u32[]{:S(2)}, u32[]{:S(2)}) collective-permute-start(bf16[64,512]{1,0:T(8,128)(2,1)} %get-tuple-element.57), channel_id=1, source_target_pairs={{12,0},{16,4},{20,8},{24,12},{28,16},{32,20},{36,24},{40,28},{44,3... | collective-permute-start | bytes 196616 | tf_op jit(solution)/shard_map/ppermute | solution.py:10
  53.0 75.1 %collective-permute-start.2 = (bf16[64,512]{1,0:T(8,128)(2,1)}, bf16[64,512]{1,0:T(8,128)(2,1)}, u32[]{:S(2)}, u32[]{:S(2)}) collective-permute-start(bf16[64,512]{1,0:T(8,128)(2,1)} %get-tuple-element.56), channel_id=1, source_target_pairs={{8,0},{12,4},{16,8},{20,12},{24,16},{28,20},{32,24},{36,28},{40,32... | collective-permute-start | bytes 196616 | tf_op jit(solution)/shard_map/ppermute | solution.py:10
  54.4 80.9 %collective-permute-start.3 = (bf16[64,512]{1,0:T(8,128)(2,1)}, bf16[64,512]{1,0:T(8,128)(2,1)}, u32[]{:S(2)}, u32[]{:S(2)}) collective-permute-start(bf16[64,512]{1,0:T(8,128)(2,1)} %get-tuple-element.55), channel_id=1, source_target_pairs={{4,0},{8,4},{12,8},{16,12},{20,16},{24,20},{28,24},{32,28},{36,32}... | collective-permute-start | bytes 196616 | tf_op jit(solution)/shard_map/ppermute | solution.py:10
  55.7 81.3 %collective-permute-start.4 = (bf16[64,512]{1,0:T(8,128)(2,1)}, bf16[64,512]{1,0:T(8,128)(2,1)}, u32[]{:S(2)}, u32[]{:S(2)}) collective-permute-start(bf16[64,512]{1,0:T(8,128)(2,1)} %get-tuple-element.54), channel_id=1, source_target_pairs={{0,4},{4,8},{8,12},{12,16},{16,20},{20,24},{24,28},{28,32},{32,36}... | collective-permute-start | bytes 196616 | tf_op jit(solution)/shard_map/ppermute | solution.py:10
  110.3 4.8 %copy-start.5 = (bf16[64,512]{1,0:T(8,128)(2,1)S(1)}, bf16[64,512]{1,0:T(8,128)(2,1)}, u32[]{:S(2)}) copy-start(bf16[64,512]{1,0:T(8,128)(2,1)} %get-tuple-element.53) | copy-start | bytes 196612
  110.3 9.8 %copy-start.4 = (bf16[64,512]{1,0:T(8,128)(2,1)S(1)}, bf16[64,512]{1,0:T(8,128)(2,1)}, u32[]{:S(2)}) copy-start(bf16[64,512]{1,0:T(8,128)(2,1)} %get-tuple-element.52) | copy-start | bytes 196612
  115.0 141.2 %reduce-scatter.3.cloned.1.call-start = ((), (), s32[]{:S(2)}) async-start(), calls=%async_computation.2 | async-start | bytes 163840 | tf_op jit(solution)/shard_map/reduce_scatter | solution.py:94
  115.0 22.8 %collective-permute-start.5 = (bf16[64,512]{1,0:T(8,128)(2,1)S(1)}, bf16[64,512]{1,0:T(8,128)(2,1)S(1)}, u32[]{:S(2)}, u32[]{:S(2)}) collective-permute-start(bf16[64,512]{1,0:T(8,128)(2,1)S(1)} %copy-done.5), channel_id=1, source_target_pairs={{0,8},{4,12},{8,16},{12,20},{16,24},{20,28},{24,32},{28,36},{32,40... | collective-permute-start | bytes 196616 | tf_op jit(solution)/shard_map/ppermute | solution.py:10
  120.1 17.7 %collective-permute-start.6 = (bf16[64,512]{1,0:T(8,128)(2,1)S(1)}, bf16[64,512]{1,0:T(8,128)(2,1)S(1)}, u32[]{:S(2)}, u32[]{:S(2)}) collective-permute-start(bf16[64,512]{1,0:T(8,128)(2,1)S(1)} %copy-done.4), channel_id=1, source_target_pairs={{0,12},{4,16},{8,20},{12,24},{16,28},{20,32},{24,36},{28,40},{32,4... | collective-permute-start | bytes 196616 | tf_op jit(solution)/shard_map/ppermute | solution.py:10
  128.1 9.7 %collective-permute-start.7 = (bf16[64,512]{1,0:T(8,128)(2,1)S(1)}, bf16[64,512]{1,0:T(8,128)(2,1)S(1)}, u32[]{:S(2)}, u32[]{:S(2)}) collective-permute-start(bf16[64,512]{1,0:T(8,128)(2,1)S(1)} %get-tuple-element.51), channel_id=1, source_target_pairs={{0,16},{4,20},{8,24},{12,28},{16,32},{20,36},{24,40},{28,44},{32,4... | collective-permute-start | bytes 196616 | tf_op jit(solution)/shard_map/ppermute | solution.py:10
Sparse Core Ops, SparseCore 0:
  115.1 31.6 reduce-scatter.4
  231.6 24.4 reduce-scatter.2
where the time goes:
time: 267 us; the launch traced here: 263 us
  local copies, waits for them, and re-layouts  99.7 us (37%)
  other arithmetic  66.1 us (25%)
  starting transfers between devices  51.7 us (19%)
  waiting for transfers between devices  24.7 us (9%)
  between operations  14.5 us (5%)
  matrix products  4.66 us (2%)
    reduce_sum x16, other arithmetic, pair_block(): return jnp.sum(inverse * source_q[:, :, None, :], axis=(1, 3))  62.8 us
    ppermute x16, starting transfers between devices, shifted(): lax.ppermute(value, axis, [(source, source + steps) for source in range(i...  51.6 us
    gather x1, local copies, waits for them, and re-layouts, per_device(): far_flat[far_index.reshape(-1)].reshape(slab_leaves, op_count * coef_count)  41.2 us
    reduce_scatter x1, waiting for transfers between devices, per_device(): lax.psum_scatter(near, 'tile', scatter_dimension=0, tiled=True)  24.6 us
    dynamic_slice x32, local copies, waits for them, and re-layouts, near_field(): lax.map(pair_block, (targets.reshape((block_count, block_leaves) + target...  15.4 us
    unnamed x40, local copies, waits for them, and re-layouts  10 us
    reshape x1, local copies, waits for them, and re-layouts, per_device(): far_flat[far_index.reshape(-1)].reshape(slab_leaves, op_count * coef_count)  9.62 us
    gather x1, local copies, waits for them, and re-layouts, per_device(): near_flat[near_index]  6.15 us
  transfers between devices with their start and end apart: 18, of which 1 were waited for; matrix products, arithmetic and copies ran while one was open for 62% of the time, Pallas kernels for 0%

commit v1 on v0

v1 whole, which is shorter than its diff:
```python
import numpy as np
import jax
import jax.numpy as jnp
from jax import lax
from jax.experimental import pallas as pl
from jax.experimental.pallas import tpu as pltpu
from jax.sharding import PartitionSpec as P

F32 = jnp.float32
BF16 = jnp.bfloat16
VM = pl.BlockSpec(memory_space=pltpu.VMEM)
SM = pl.BlockSpec(memory_space=pltpu.SMEM)

def dot(a, b, dims=((1,), (0,))):
    return lax.dot_general(a, b, (dims, ((), ())), preferred_element_type=F32)


def pack_kernel(pos_ref, charge_ref, count_ref, multi_ref, leaf_ref, far_ref, *out_refs):
    peers, cap = leaf_ref.shape
    capm = far_ref.shape[1]
    leaves, lanes = charge_ref.shape
    lane = lax.broadcasted_iota(jnp.int32, (leaves, lanes), 1)
    live = lane < count_ref[...]
    masked = jnp.where(live, charge_ref[...].astype(F32), 0.0).astype(BF16)
    table = jnp.concatenate([pos_ref[0], pos_ref[1], pos_ref[2], masked], axis=1)
    box = lax.broadcasted_iota(jnp.int32, (leaves, cap), 0)
    boxm = lax.broadcasted_iota(jnp.int32, (leaves, capm), 0)
    multi = multi_ref[...]
    for k in range(peers):
        pick = jnp.where(box == leaf_ref[k:k + 1, :], 1.0, 0.0).astype(BF16)
        rows = dot(pick, table, ((0,), (0,))).astype(BF16)
        for c in range(4):
            out_refs[k][c * cap:(c + 1) * cap, :] = rows[:, c * lanes:(c + 1) * lanes]
        pickm = jnp.where(boxm == far_ref[k:k + 1, :], 1.0, 0.0).astype(BF16)
        out_refs[k][4 * cap:4 * cap + capm, :] = dot(pickm, multi, ((0,), (0,))).astype(BF16)


def near_kernel(slot_ref, count_ref, pos_ref, perm_s_ref, perm_t_ref, *refs):
    got = refs[:9]
    out_ref, w_ref, q_ref, lhs_ref = refs[9:]
    leaves, lanes = out_ref.shape
    columns = slot_ref.shape[0]
    cap = 64
    slots = 9 * cap
    one = jnp.ones((16, lanes), BF16)
    zero = jnp.zeros((16, lanes), BF16)

    def split(x, y, z, bias):
        x, y, z = x.astype(F32), y.astype(F32), z.astype(F32)
        total = x * x + y * y + z * z + bias
        hi = total.astype(BF16)
        rest = total - hi.astype(F32)
        mid = rest.astype(BF16)
        return hi, mid, (rest - mid.astype(F32)).astype(BF16)

    for k in range(9):
        for g in range(cap // 16):
            x, y, z, q = [got[k][c * cap + g * 16:c * cap + g * 16 + 16, :] for c in range(4)]
            hi, mid, lo = split(x, y, z, 0.09)
            stack = jnp.concatenate([x, y, z, hi, mid, lo, one, zero], axis=0)
            tiles = dot(perm_s_ref[...], stack).astype(BF16)
            w_ref[k * cap + g * 16:k * cap + g * 16 + 16] = tiles.reshape(16, 16, lanes)
            q_ref[k * cap + g * 16:k * cap + g * 16 + 16, :] = q.astype(F32)
    w_ref[slots] = one
    q_ref[slots:slots + 8, :] = jnp.zeros((8, lanes), F32)

    for g in range(leaves // 16):
        x, y, z = [pos_ref[c, g * 16:g * 16 + 16, :] for c in range(3)]
        hi, mid, lo = split(x, y, z, 0.0)
        stack = jnp.concatenate([x, y, z, hi, mid, lo, one, zero], axis=0)
        feat = dot(stack, perm_t_ref[...], ((0,), (0,)))
        for j in range(8):
            lhs_ref[g * 8 + j] = feat[:, j * 32:j * 32 + 32].astype(BF16)

    lane_row = lax.broadcasted_iota(jnp.int32, (1, lanes), 1)

    def pair(p, _):
        l0 = 2 * p
        tiles = []
        charge = []
        for a in range(2):
            for n in range(columns):
                s = slot_ref[n, l0 + a]
                s = jnp.where(s < 0, slots, s)
                t = w_ref[s]
                tiles.append(jnp.concatenate([t, zero] if a == 0 else [zero, t], axis=0))
                charge.append(q_ref[pl.ds(s, 1), :])
        r2 = dot(lhs_ref[p], jnp.concatenate(tiles, axis=1))
        inv = lax.rsqrt(r2)
        for a in range(2):
            acc = jnp.zeros((lanes, lanes), F32)
            for n in range(columns):
                i = a * columns + n
                acc = acc + inv[:, i * lanes:(i + 1) * lanes] * charge[i]
            row = jnp.sum(acc.T, axis=0, keepdims=True)
            row = jnp.where(lane_row < count_ref[l0 + a], row, 0.0)
            out_ref[pl.ds(l0 + a, 1), :] = row
        return 0

    lax.fori_loop(0, leaves // 2, pair, 0, unroll=2)


def perms():
    s = np.zeros((256, 128), np.float32)
    t = np.zeros((128, 256), np.float32)
    plane_s = [(0, -2.0), (1, -2.0), (2, -2.0), (3, 1.0), (4, 1.0), (5, 1.0), (6, 1.0), (6, 1.0), (6, 1.0)]
    plane_t = [(0, 1.0), (1, 1.0), (2, 1.0), (6, 1.0), (6, 1.0), (6, 1.0), (3, 1.0), (4, 1.0), (5, 1.0)]
    for j in range(16):
        for p, (plane, v) in enumerate(plane_s):
            s[16 * j + p, plane * 16 + j] = v
        for p, (plane, v) in enumerate(plane_t):
            t[plane * 16 + j, 16 * j + p] = v
    return jnp.asarray(s, BF16), jnp.asarray(t, BF16)


def far_kernel(tile_ref, slot_ref, m2l_ref, near_ref, *refs):
    got = refs[:9]
    part_refs = refs[9:13]
    out_ref, table_ref, hot_ref = refs[13:]
    ops, leaves = slot_ref.shape
    capm = 192
    lanes = out_ref.shape[1]
    half = table_ref.shape[0]
    table_ref[...] = jnp.zeros_like(table_ref)
    for k in range(9):
        for h in range(2):
            lo, hi = max(k * capm, h * half), min((k + 1) * capm, (h + 1) * half)
            if lo < hi:
                table_ref[lo - h * half:hi - h * half, h * lanes:(h + 1) * lanes] = \
                    got[k][256 + lo - k * capm:256 + hi - k * capm, :]
    out_ref[...] = jnp.zeros_like(out_ref)
    lane0 = lax.broadcasted_iota(jnp.int32, (leaves, lanes), 1)
    iota0 = lane0.astype(F32).astype(BF16)
    iota1 = (lane0 + lanes).astype(F32).astype(BF16)
    one = jnp.ones((leaves, lanes), BF16)
    zero = jnp.zeros((leaves, lanes), BF16)

    def chunk(start, n):
        st = slot_ref[pl.ds(start, n), :].astype(F32)
        if n < 8:
            st = jnp.concatenate([st, jnp.full((8 - n, leaves), -1.0, F32)], axis=0)
        st = st.T
        halves = []
        for i in range(n):
            col = jnp.broadcast_to(st[:, i:i + 1], (leaves, lanes))
            upper = col >= half
            halves.append(upper)
            kk = jnp.where(upper, col - half, col)
            for j in range(half // 256):
                v = (kk - 256.0 * j).astype(BF16)
                hot_ref[i * leaves:(i + 1) * leaves, j * 256:j * 256 + 128] = jnp.where(v == iota0, one, zero)
                hot_ref[i * leaves:(i + 1) * leaves, j * 256 + 128:j * 256 + 256] = jnp.where(v == iota1, one, zero)
        both = dot(hot_ref[:n * leaves, :], table_ref[...])
        rows = []
        for i in range(n):
            b = both[i * leaves:(i + 1) * leaves]
            rows.append(jnp.where(halves[i], b[:, lanes:], b[:, :lanes]).astype(BF16))
        mats = m2l_ref[pl.ds(start, n)].reshape(n * lanes, lanes)
        out_ref[...] += dot(jnp.concatenate(rows, axis=1), mats)

    full = ops // 8

    def body(c, _):
        chunk(pl.multiple_of(c * 8, 8), 8)
        return 0

    lax.fori_loop(0, full, body, 0)
    if ops % 8:
        chunk(full * 8, ops % 8)
    rows = leaves // 4
    for d in range(4):
        at = pl.multiple_of(lax.rem(tile_ref[0] + d, 4) * rows, rows)
        part_refs[d][:, :lanes] = near_ref[pl.ds(at, rows), :]
        part_refs[d][:, lanes:] = out_ref[pl.ds(at, rows), :]


def params(mb=24):
    return pltpu.CompilerParams(vmem_limit_bytes=mb * 1024 * 1024)


def pack(pos, charges, counts, multi, leaf_send, far_send):
    peers, cap = leaf_send.shape
    capm = far_send.shape[1]
    return pl.pallas_call(
        pack_kernel, out_shape=[jax.ShapeDtypeStruct((4 * cap + capm, 128), BF16)] * peers,
        in_specs=[VM] * 6, out_specs=[VM] * peers, compiler_params=params(),
    )(pos, charges, counts[:, None], multi, leaf_send, far_send)


def near(slots_t, counts, pos, got):
    s, t = perms()
    return pl.pallas_call(
        near_kernel, out_shape=jax.ShapeDtypeStruct((256, 128), F32),
        in_specs=[SM, SM] + [VM] * (3 + len(got)), out_specs=VM,
        scratch_shapes=[pltpu.VMEM((577, 16, 128), BF16), pltpu.VMEM((584, 128), F32), pltpu.VMEM((128, 128, 32), BF16)],
        compiler_params=params(),
    )(slots_t, counts, pos, s, t, *got)


def far(tile, slots_t, m2l, near_part, got):
    return pl.pallas_call(
        far_kernel, out_shape=[jax.ShapeDtypeStruct((64, 256), F32)] * 4,
        in_specs=[SM] + [VM] * (3 + len(got)), out_specs=[VM] * 4,
        scratch_shapes=[pltpu.VMEM((256, 128), F32), pltpu.VMEM((1024, 256), BF16), pltpu.VMEM((2048, 1024), BF16)],
        compiler_params=params(),
    )(tile, slots_t, m2l, near_part, *got)


def per_device(positions, charges, leaf_counts, multipoles, m2l_ops, leaf_send, pair_slots, far_send, far_slots):
    peers = leaf_send.shape[0]
    reach = (peers - 1) // 2
    slabs = lax.axis_size("slab")
    tiles = lax.axis_size("tile")
    planes = jnp.transpose(positions, (1, 0, 2))
    payload = pack(planes, charges, leaf_counts, multipoles, leaf_send, far_send)
    got = list(payload)
    for step in range(reach, 0, -1):
        for k in (reach + step, reach - step):
            hops = k - reach
            got[k] = lax.ppermute(payload[k], "slab", [(s, (s + hops) % slabs) for s in range(slabs)])
    near_part = near(pair_slots.T, leaf_counts, planes, got)
    tile = lax.axis_index("tile").astype(jnp.int32).reshape(1)
    parts = far(tile, far_slots.T, m2l_ops, near_part, got)
    total = parts[0]
    for step in range(1, tiles):
        total = total + lax.ppermute(parts[step], "tile", [(t, (t + step) % tiles) for t in range(tiles)])
    return total[:, :128], total[:, 128:]


def solution(mesh):
    return jax.shard_map(
        per_device,
        mesh=mesh,
        in_specs=(
            P("slab", None, None),
            P("slab", None),
            P("slab"),
            P("slab", None),
            P("tile", None, None),
            P("slab", "tile"),
            P("slab", "tile"),
            P("slab", "tile"),
            P("slab", "tile"),
        ),
        out_specs=(P(("slab", "tile"), None), P(("slab", "tile"), None)),
        check_vma=False,
    )
```

time: 267 us -> 111 us (0.42)
  local copies, waits for them, and re-layouts: 99.7 us -> 12 us
  other arithmetic: 66.1 us -> 0.02 us
  Pallas kernels: 0 us -> 57.5 us
  starting transfers between devices: 51.7 us -> 13.6 us
  between operations: 14.5 us -> 0.69 us
  matrix products: 4.66 us -> 0 us
    reduce_sum x16 -> x0, other arithmetic: 62.8 us -> none  [pair_block(): return jnp.sum(inverse * source_q[:, :, None, :], axis=(1, 3))]
    pallas_call x0 -> x3, Pallas kernels: none -> 57.5 us  [the longest x1 33.1 us: near(): pl.pallas_call(near_kernel, out_shape=jax.ShapeDtypeStruct((256, 128), F3...]
    gather x4 -> x0, local copies, waits for them, and re-layouts: 54.8 us -> none  [the longest x1 41.2 us: per_device(): far_flat[far_index.reshape(-1)].reshape(slab_leaves, op_count * coef_count)]
    ppermute x16 -> x11, starting transfers between devices: 51.6 us -> 13.6 us  [the longest x8 10.7 us: per_device(): lax.ppermute(payload[k], 'slab', [(s, (s + hops) % slabs) for s in range(...]
    ppermute x16 -> x11, waiting for transfers between devices: 0.04 us -> 25.2 us  [the longest x8 19.7 us: per_device(): lax.ppermute(payload[k], 'slab', [(s, (s + hops) % slabs) for s in range(...]
    reduce_scatter x2 -> x0, waiting for transfers between devices: 24.6 us -> none  [the longest x1 24.6 us: per_device(): lax.psum_scatter(near, 'tile', scatter_dimension=0, tiled=True)]
    dynamic_slice x32 -> x0, local copies, waits for them, and re-layouts: 15.4 us -> none  [near_field(): lax.map(pair_block, (targets.reshape((block_count, block_leaves) + target...]
    reshape x2 -> x0, local copies, waits for them, and re-layouts: 9.88 us -> none  [the longest x1 9.62 us: per_device(): far_flat[far_index.reshape(-1)].reshape(slab_leaves, op_count * coef_count)]
  transfers between devices with their start and end apart: 18 -> 11, of which waited for: 1 -> 10; matrix products, arithmetic and copies ran while one was open for 62% -> 0% of each run, Pallas kernels for 0% -> 0%
where the time goes in v1:
time: 111 us; the launch traced here: 109 us
  Pallas kernels  57.5 us (52%)
  waiting for transfers between devices  25.2 us (23%)
  starting transfers between devices  13.6 us (12%)
  local copies, waits for them, and re-layouts  12 us (11%)
    pallas_call x1, Pallas kernels, near(): pl.pallas_call(near_kernel, out_shape=jax.ShapeDtypeStruct((256, 128), F3...  33.1 us
    pallas_call x1, Pallas kernels, far(): pl.pallas_call(far_kernel, out_shape=[jax.ShapeDtypeStruct((64, 256), F32...  23.7 us
    ppermute x8, waiting for transfers between devices, per_device(): lax.ppermute(payload[k], 'slab', [(s, (s + hops) % slabs) for s in range(...  19.7 us
    ppermute x8, starting transfers between devices, per_device(): lax.ppermute(payload[k], 'slab', [(s, (s + hops) % slabs) for s in range(...  10.7 us
    unnamed x24, local copies, waits for them, and re-layouts  10.6 us
    ppermute x3, waiting for transfers between devices, per_device(): lax.ppermute(parts[step], 'tile', [(t, (t + step) % tiles) for t in range...  5.47 us
    ppermute x3, starting transfers between devices, per_device(): lax.ppermute(parts[step], 'tile', [(t, (t + step) % tiles) for t in range...  2.93 us
  transfers between devices with their start and end apart: 11, of which 10 were waited for; matrix products, arithmetic and copies ran while one was open for 0% of the time, Pallas kernels for 0%

profile of v1, /device:TPU:6, one launch (start us, length us, event | category | flops | bytes accessed | tf_op | source)
XLA Modules:
  0.0 109.1 jit_solution(2543580692532622492)
XLA Ops:
  0.6 0.8 copy.13.count_ref
  1.4 0.0 copy-start.1
  1.5 0.9 copy-done.1
  2.4 0.0 copy-start.6
  2.4 0.8 copy-done.6
  3.2 0.0 copy-start.7
  3.2 0.8 copy-done.7
  4.1 0.0 copy-start.8
  4.1 0.7 copy-done.8
  4.8 0.0 copy-start.9
  4.8 0.7 copy-done.9
  5.5 0.7 shard_map.122
  6.2 8.8 %collective-permute-start = (bf16[448,128]{1,0:T(8,128)(2,1)S(1)}, bf16[448,128]{1,0:T(8,128)(2,1)S(1)}, u32[]{:S(2)}, u32[]{:S(2)}) collective-permute-start(bf16[448,128]{1,0:T(8,128)(2,1)S(1)} %get-tuple-element.15), channel_id=1, source_target_pairs={{0,240},{4,244},{8,248},{12,252},{16,0},{20,4},{24,8},{28,12},{32,... | collective-permute-start | bytes 344072 | tf_op jit(solution)/shard_map/ppermute | solution.py:220
  15.0 0.6 collective-permute-start.1
  15.7 0.4 collective-permute-start.2
  16.1 0.7 collective-permute-start.3
  16.8 0.1 collective-permute-start.4
  16.9 3.7 %collective-permute-done.refs_0_ = bf16[448,128]{1,0:T(8,128)(2,1)S(1)} collective-permute-done((bf16[448,128]{1,0:T(8,128)(2,1)S(1)}, bf16[448,128]{1,0:T(8,128)(2,1)S(1)}, u32[]{:S(2)}, u32[]{:S(2)}) %collective-permute-start) | collective-permute-done | bytes 114720 | tf_op jit(solution)/shard_map/ppermute | solution.py:220
  20.6 0.0 collective-permute-start.5
  20.6 3.5 %collective-permute-done.1.refs_1_ = bf16[448,128]{1,0:T(8,128)(2,1)S(1)} collective-permute-done((bf16[448,128]{1,0:T(8,128)(2,1)S(1)}, bf16[448,128]{1,0:T(8,128)(2,1)S(1)}, u32[]{:S(2)}, u32[]{:S(2)}) %collective-permute-start.1) | collective-permute-done | bytes 114720 | tf_op jit(solution)/shard_map/ppermute | solution.py:220
  24.2 0.0 collective-permute-start.6
  24.2 1.9 %collective-permute-done.2.refs_2_ = bf16[448,128]{1,0:T(8,128)(2,1)S(1)} collective-permute-done((bf16[448,128]{1,0:T(8,128)(2,1)S(1)}, bf16[448,128]{1,0:T(8,128)(2,1)S(1)}, u32[]{:S(2)}, u32[]{:S(2)}) %collective-permute-start.2) | collective-permute-done | bytes 114720 | tf_op jit(solution)/shard_map/ppermute | solution.py:220
  26.1 0.0 collective-permute-start.7
  26.1 1.2 %collective-permute-done.3.refs_3_ = bf16[448,128]{1,0:T(8,128)(2,1)S(1)} collective-permute-done((bf16[448,128]{1,0:T(8,128)(2,1)S(1)}, bf16[448,128]{1,0:T(8,128)(2,1)S(1)}, u32[]{:S(2)}, u32[]{:S(2)}) %collective-permute-start.3) | collective-permute-done | bytes 114720 | tf_op jit(solution)/shard_map/ppermute | solution.py:220
  27.3 0.0 collective-permute-done.4.refs_5_
  27.3 1.5 %collective-permute-done.5.refs_6_ = bf16[448,128]{1,0:T(8,128)(2,1)S(1)} collective-permute-done((bf16[448,128]{1,0:T(8,128)(2,1)S(1)}, bf16[448,128]{1,0:T(8,128)(2,1)S(1)}, u32[]{:S(2)}, u32[]{:S(2)}) %collective-permute-start.5) | collective-permute-done | bytes 114720 | tf_op jit(solution)/shard_map/ppermute | solution.py:220
  28.7 4.9 %collective-permute-done.6.refs_7_ = bf16[448,128]{1,0:T(8,128)(2,1)S(1)} collective-permute-done((bf16[448,128]{1,0:T(8,128)(2,1)S(1)}, bf16[448,128]{1,0:T(8,128)(2,1)S(1)}, u32[]{:S(2)}, u32[]{:S(2)}) %collective-permute-start.6) | collective-permute-done | bytes 114720 | tf_op jit(solution)/shard_map/ppermute | solution.py:220
  33.7 3.0 %collective-permute-done.7.refs_8_ = bf16[448,128]{1,0:T(8,128)(2,1)S(1)} collective-permute-done((bf16[448,128]{1,0:T(8,128)(2,1)S(1)}, bf16[448,128]{1,0:T(8,128)(2,1)S(1)}, u32[]{:S(2)}, u32[]{:S(2)}) %collective-permute-start.7) | collective-permute-done | bytes 114720 | tf_op jit(solution)/shard_map/ppermute | solution.py:220
  36.6 0.0 copy-start.2
  36.6 0.9 copy-done.2
  37.6 0.0 copy-start.4
  37.6 0.8 copy-done.4
  38.4 0.0 copy-start.5
  38.4 0.8 copy-done.5
  39.2 0.7 copy-done.10
  39.9 0.7 copy-done.11
  40.6 33.1 %shard_map.123.near_ref = f32[256,128]{1,0:T(8,128)S(1)} custom-call(s32[7,256]{1,0:T(8,128)S(1)} %bitcast.8, s32[256]{0:T(256)S(1)} %copy-done.11, bf16[3,256,128]{2,1,0:T(8,128)(2,1)S(1)} %bitcast.6, bf16[256,128]{1,0:T(8,128)(2,1)S(1)} %copy-done.5, bf16[128,256]{1,0:T(8,128)(2,1)S(1)} %copy-done.4, bf16[448,128]{1,0:T(8,128)(2,1)S(1)} %collective-permute-done.refs_0_, ...), custom_call_target="tpu_custom_call" | custom-call | tf_op jit(solution)/shard_map/pallas_call | solution.py:192
  73.7 0.0 copy-start
  73.7 1.7 %copy-done = bf16[79,128,128]{2,1,0:T(8,128)(2,1)S(1)} copy-done((bf16[79,128,128]{2,1,0:T(8,128)(2,1)S(1)}, bf16[79,128,128]{2,1,0:T(8,128)(2,1)}, u32[]{:S(2)}) %copy-start) | copy-done | bytes 2588696
  75.5 0.9 copy-done.3
  76.4 23.7 %shard_map.124 = (f32[64,256]{1,0:T(8,128)S(1)}, f32[64,256]{1,0:T(8,128)S(1)}, f32[64,256]{1,0:T(8,128)S(1)}, f32[64,256]{1,0:T(8,128)S(1)}) custom-call(s32[1]{0:T(128)} %bitcast.tile_ref, s32[79,256]{1,0:T(8,128)S(1)} %bitcast.7, bf16[79,128,128]{2,1,0:T(8,128)(2,1)S(1)} %copy-done, f32[256,128]{1,0:T(8,128)S(1)} %shard_map.123.near_ref, ...), custom_call_target="tpu_custom_call" | custom-call | tf_op jit(solution)/shard_map/pallas_call | solution.py:201
  100.0 0.5 collective-permute-start.8
  100.5 2.4 %collective-permute-start.9 = (f32[64,256]{1,0:T(8,128)S(1)}, f32[64,256]{1,0:T(8,128)S(1)}, u32[]{:S(2)}, u32[]{:S(2)}) collective-permute-start(f32[64,256]{1,0:T(8,128)S(1)} %get-tuple-element.26), channel_id=1, source_target_pairs={{0,2},{1,3},{2,0},{3,1},{4,6},{5,7},{6,4},{7,5},{8,10},{9,11},{10,... | collective-permute-start | bytes 196616 | tf_op jit(solution)/shard_map/ppermute | solution.py:226
  102.9 0.0 collective-permute-start.10
  103.0 1.7 %collective-permute-done.8 = f32[64,256]{1,0:T(8,128)S(1)} collective-permute-done((f32[64,256]{1,0:T(8,128)S(1)}, f32[64,256]{1,0:T(8,128)S(1)}, u32[]{:S(2)}, u32[]{:S(2)}) %collective-permute-start.8) | collective-permute-done | bytes 65568 | tf_op jit(solution)/shard_map/ppermute | solution.py:226
  104.7 1.8 %collective-permute-done.9 = f32[64,256]{1,0:T(8,128)S(1)} collective-permute-done((f32[64,256]{1,0:T(8,128)S(1)}, f32[64,256]{1,0:T(8,128)S(1)}, u32[]{:S(2)}, u32[]{:S(2)}) %collective-permute-start.9) | collective-permute-done | bytes 65568 | tf_op jit(solution)/shard_map/ppermute | solution.py:226
  106.5 1.9 %collective-permute-done.10 = f32[64,256]{1,0:T(8,128)S(1)} collective-permute-done((f32[64,256]{1,0:T(8,128)S(1)}, f32[64,256]{1,0:T(8,128)S(1)}, u32[]{:S(2)}, u32[]{:S(2)}) %collective-permute-start.10) | collective-permute-done | bytes 65568 | tf_op jit(solution)/shard_map/ppermute | solution.py:226
  108.4 0.6 fusion
  (4 shorter events, 0.0 us)
Async XLA Ops:
  1.4 0.9 copy-start.1
  2.4 0.8 copy-start.6
  3.2 0.8 copy-start.7
  4.1 0.7 copy-start.8
  4.8 0.7 copy-start.9
  6.2 14.4 %collective-permute-start = (bf16[448,128]{1,0:T(8,128)(2,1)S(1)}, bf16[448,128]{1,0:T(8,128)(2,1)S(1)}, u32[]{:S(2)}, u32[]{:S(2)}) collective-permute-start(bf16[448,128]{1,0:T(8,128)(2,1)S(1)} %get-tuple-element.15), channel_id=1, source_target_pairs={{0,240},{4,244},{8,248},{12,252},{16,0},{20,4},{24,8},{28,12},{32,... | collective-permute-start | bytes 344072 | tf_op jit(solution)/shard_map/ppermute | solution.py:220
  15.0 9.1 %collective-permute-start.1 = (bf16[448,128]{1,0:T(8,128)(2,1)S(1)}, bf16[448,128]{1,0:T(8,128)(2,1)S(1)}, u32[]{:S(2)}, u32[]{:S(2)}) collective-permute-start(bf16[448,128]{1,0:T(8,128)(2,1)S(1)} %get-tuple-element.16), channel_id=1, source_target_pairs={{0,244},{4,248},{8,252},{12,0},{16,4},{20,8},{24,12},{28,16},{32,2... | collective-permute-start | bytes 344072 | tf_op jit(solution)/shard_map/ppermute | solution.py:220
  15.7 10.4 %collective-permute-start.2 = (bf16[448,128]{1,0:T(8,128)(2,1)S(1)}, bf16[448,128]{1,0:T(8,128)(2,1)S(1)}, u32[]{:S(2)}, u32[]{:S(2)}) collective-permute-start(bf16[448,128]{1,0:T(8,128)(2,1)S(1)} %get-tuple-element.17), channel_id=1, source_target_pairs={{0,248},{4,252},{8,0},{12,4},{16,8},{20,12},{24,16},{28,20},{32,24... | collective-permute-start | bytes 344072 | tf_op jit(solution)/shard_map/ppermute | solution.py:220
  16.1 11.2 %collective-permute-start.3 = (bf16[448,128]{1,0:T(8,128)(2,1)S(1)}, bf16[448,128]{1,0:T(8,128)(2,1)S(1)}, u32[]{:S(2)}, u32[]{:S(2)}) collective-permute-start(bf16[448,128]{1,0:T(8,128)(2,1)S(1)} %get-tuple-element.18), channel_id=1, source_target_pairs={{0,252},{4,0},{8,4},{12,8},{16,12},{20,16},{24,20},{28,24},{32,28}... | collective-permute-start | bytes 344072 | tf_op jit(solution)/shard_map/ppermute | solution.py:220
  16.8 10.5 %collective-permute-start.4 = (bf16[448,128]{1,0:T(8,128)(2,1)S(1)}, bf16[448,128]{1,0:T(8,128)(2,1)S(1)}, u32[]{:S(2)}, u32[]{:S(2)}) collective-permute-start(bf16[448,128]{1,0:T(8,128)(2,1)S(1)} %get-tuple-element.20), channel_id=1, source_target_pairs={{0,4},{4,8},{8,12},{12,16},{16,20},{20,24},{24,28},{28,32},{32,36}... | collective-permute-start | bytes 344072 | tf_op jit(solution)/shard_map/ppermute | solution.py:220
  20.6 8.1 %collective-permute-start.5 = (bf16[448,128]{1,0:T(8,128)(2,1)S(1)}, bf16[448,128]{1,0:T(8,128)(2,1)S(1)}, u32[]{:S(2)}, u32[]{:S(2)}) collective-permute-start(bf16[448,128]{1,0:T(8,128)(2,1)S(1)} %get-tuple-element.21), channel_id=1, source_target_pairs={{0,8},{4,12},{8,16},{12,20},{16,24},{20,28},{24,32},{28,36},{32,40... | collective-permute-start | bytes 344072 | tf_op jit(solution)/shard_map/ppermute | solution.py:220
  24.2 9.5 %collective-permute-start.6 = (bf16[448,128]{1,0:T(8,128)(2,1)S(1)}, bf16[448,128]{1,0:T(8,128)(2,1)S(1)}, u32[]{:S(2)}, u32[]{:S(2)}) collective-permute-start(bf16[448,128]{1,0:T(8,128)(2,1)S(1)} %get-tuple-element.22), channel_id=1, source_target_pairs={{0,12},{4,16},{8,20},{12,24},{16,28},{20,32},{24,36},{28,40},{32,4... | collective-permute-start | bytes 344072 | tf_op jit(solution)/shard_map/ppermute | solution.py:220
  26.1 10.6 %collective-permute-start.7 = (bf16[448,128]{1,0:T(8,128)(2,1)S(1)}, bf16[448,128]{1,0:T(8,128)(2,1)S(1)}, u32[]{:S(2)}, u32[]{:S(2)}) collective-permute-start(bf16[448,128]{1,0:T(8,128)(2,1)S(1)} %get-tuple-element.23), channel_id=1, source_target_pairs={{0,16},{4,20},{8,24},{12,28},{16,32},{20,36},{24,40},{28,44},{32,4... | collective-permute-start | bytes 344072 | tf_op jit(solution)/shard_map/ppermute | solution.py:220
  36.6 0.9 copy-start.2
  37.6 0.8 copy-start.4
  38.4 0.8 copy-start.5
  39.2 0.7 copy-start.10
  39.9 0.7 copy-start.11
  73.7 1.7 %copy-start = (bf16[79,128,128]{2,1,0:T(8,128)(2,1)S(1)}, bf16[79,128,128]{2,1,0:T(8,128)(2,1)}, u32[]{:S(2)}) copy-start(bf16[79,128,128]{2,1,0:T(8,128)(2,1)} %m2l_ref.1) | copy-start | bytes 7766020
  75.5 0.9 copy-start.3
  100.0 4.7 %collective-permute-start.8 = (f32[64,256]{1,0:T(8,128)S(1)}, f32[64,256]{1,0:T(8,128)S(1)}, u32[]{:S(2)}, u32[]{:S(2)}) collective-permute-start(f32[64,256]{1,0:T(8,128)S(1)} %get-tuple-element.25), channel_id=1, source_target_pairs={{0,1},{1,2},{2,3},{3,0},{4,5},{5,6},{6,7},{7,4},{8,9},{9,10},{10,1... | collective-permute-start | bytes 196616 | tf_op jit(solution)/shard_map/ppermute | solution.py:226
  100.5 6.0 %collective-permute-start.9 = (f32[64,256]{1,0:T(8,128)S(1)}, f32[64,256]{1,0:T(8,128)S(1)}, u32[]{:S(2)}, u32[]{:S(2)}) collective-permute-start(f32[64,256]{1,0:T(8,128)S(1)} %get-tuple-element.26), channel_id=1, source_target_pairs={{0,2},{1,3},{2,0},{3,1},{4,6},{5,7},{6,4},{7,5},{8,10},{9,11},{10,... | collective-permute-start | bytes 196616 | tf_op jit(solution)/shard_map/ppermute | solution.py:226
  102.9 5.5 %collective-permute-start.10 = (f32[64,256]{1,0:T(8,128)S(1)}, f32[64,256]{1,0:T(8,128)S(1)}, u32[]{:S(2)}, u32[]{:S(2)}) collective-permute-start(f32[64,256]{1,0:T(8,128)S(1)} %get-tuple-element.27), channel_id=1, source_target_pairs={{0,3},{1,0},{2,1},{3,2},{4,7},{5,4},{6,5},{7,6},{8,11},{9,8},{10,9... | collective-permute-start | bytes 196616 | tf_op jit(solution)/shard_map/ppermute | solution.py:226

commit v2 on v0

v2 whole, which is shorter than its diff:
```python
import jax
import jax.numpy as jnp
from jax import lax
from jax.experimental import pallas as pl
from jax.experimental.pallas import tpu as pltpu
from jax.sharding import PartitionSpec as P

F32 = jnp.float32
BF16 = jnp.bfloat16
I32 = jnp.int32
PEERS, CAP, CAPM = 9, 64, 192
LEAVES, LANES = 256, 128
COLUMNS, OPS = 7, 79
SLOTS = PEERS * CAP
CHUNK = 16
CHUNKS = 5
TABLE = 1024
HBM = pl.BlockSpec(memory_space=pltpu.HBM)
VM = pl.BlockSpec(memory_space=pltpu.VMEM)
SM = pl.BlockSpec(memory_space=pltpu.SMEM)


def dot(a, b, dims=((1,), (0,))):
    return lax.dot_general(a, b, (dims, ((), ())), preferred_element_type=F32)


def iota(shape, dim):
    return lax.broadcasted_iota(I32, shape, dim)


def fetch(pairs, sems):
    copies = [pltpu.make_async_copy(a, b, sems.at[i]) for i, (a, b) in enumerate(pairs)]
    for c in copies:
        c.start()
    return copies


def params(mb):
    return pltpu.CompilerParams(vmem_limit_bytes=mb * 1024 * 1024)


def column(row):
    return jnp.broadcast_to(row.astype(F32), (8, LEAVES)).T[:, 0:1]


def pack_kernel(pos_h, charge_h, count_h, multi_h, leaf_h, far_h, *refs):
    out_refs = refs[:PEERS]
    pos, charge, count, multi_ref, leaf, far_s, sems = refs[PEERS:]
    for c in fetch([(pos_h, pos), (charge_h, charge), (count_h, count), (multi_h, multi_ref), (leaf_h, leaf), (far_h, far_s)], sems):
        c.wait()
    live = iota((LEAVES, LANES), 1).astype(F32) < column(count[...])
    masked = jnp.where(live, charge[...].astype(F32), 0.0).astype(BF16)
    table = jnp.concatenate([pos[0], pos[1], pos[2], masked], axis=1)
    box = iota((LEAVES, CAP), 0)
    boxm = iota((LEAVES, CAPM), 0)
    multi = multi_ref[...]
    for k in range(PEERS):
        pick = jnp.where(box == leaf[k:k + 1, :], 1.0, 0.0).astype(BF16)
        rows = dot(pick, table, ((0,), (0,))).astype(BF16)
        for c in range(4):
            out_refs[k][c * CAP:(c + 1) * CAP, :] = rows[:, c * LANES:(c + 1) * LANES]
        pickm = jnp.where(boxm == far_s[k:k + 1, :], 1.0, 0.0).astype(BF16)
        out_refs[k][4 * CAP:4 * CAP + CAPM, :] = dot(pickm, multi, ((0,), (0,))).astype(BF16)


def pack(planes, charges, count_row, multi, leaf_send, far_send):
    return pl.pallas_call(
        pack_kernel,
        out_shape=[jax.ShapeDtypeStruct((4 * CAP + CAPM, LANES), BF16)] * PEERS,
        in_specs=[HBM] * 6,
        out_specs=[VM] * PEERS,
        scratch_shapes=[
            pltpu.VMEM((3, LEAVES, LANES), BF16), pltpu.VMEM((LEAVES, LANES), BF16), pltpu.VMEM((1, LEAVES), I32),
            pltpu.VMEM((LEAVES, LANES), BF16), pltpu.VMEM((PEERS, CAP), I32), pltpu.VMEM((PEERS, CAPM), I32),
            pltpu.SemaphoreType.DMA((6,)),
        ],
        compiler_params=params(56),
        name="pack",
    )(planes, charges, count_row, multi, leaf_send, far_send)


def squares(x, y, z, bias):
    x, y, z = x.astype(F32), y.astype(F32), z.astype(F32)
    total = x * x + y * y + z * z + bias
    hi = total.astype(BF16)
    rest = total - hi.astype(F32)
    mid = rest.astype(BF16)
    return hi, mid, (rest - mid.astype(F32)).astype(BF16)


def spread(transposed, scale, order):
    shape = (128, 256) if transposed else (256, 128)
    big, small = iota(shape, 1 if transposed else 0), iota(shape, 0 if transposed else 1)
    feature, item = big & 15, big >> 4
    plane, item2 = small >> 4, small & 15
    value = jnp.zeros(shape, F32)
    for f, (p, v) in enumerate(order):
        value = jnp.where((feature == f) & (plane == p), v * scale if p < 3 else v, value)
    return jnp.where(item == item2, value, 0.0).astype(BF16)


def prep_kernel(pos_h, count_h, slot_h, pair_h, own_h, lhs_ref, order_ref, code_ref, base_ref, pair_ref, own_ref, pos, count, slot, pair, sems):
    copies = fetch([(pos_h, pos), (count_h, count), (slot_h, slot), (pair_h, pair), (own_h, own_ref)], sems)
    for c in copies:
        c.wait()
    leaf_row = iota((1, LEAVES), 1).astype(F32)
    key_row = count[...].astype(F32) * LEAVES + leaf_row
    key_col = jnp.broadcast_to(key_row, (8, LEAVES)).T[:, 0:1]
    rank = jnp.sum(jnp.where(key_col > key_row, 1.0, 0.0), axis=0, keepdims=True)
    move = jnp.where(rank == iota((LEAVES, LEAVES), 0).astype(F32), 1.0, 0.0).astype(BF16)
    order_ref[...] = dot(jnp.broadcast_to(leaf_row, (8, LEAVES)).astype(BF16), move, ((1,), (1,))).astype(I32)
    pair_ref[:COLUMNS, :] = jnp.where(pair[...] < 0, SLOTS, pair[...])
    pair_ref[COLUMNS:, :] = count[...]
    x, y, z = [dot(move, pos[c]).astype(BF16) for c in range(3)]
    hi, mid, lo = squares(x, y, z, 0.0)
    one = jnp.ones((16, LANES), BF16)
    zero = jnp.zeros((16, LANES), BF16)
    layout = spread(True, 1.0, [(0, 1.0), (1, 1.0), (2, 1.0), (6, 1.0), (6, 1.0), (6, 1.0), (3, 1.0), (4, 1.0), (5, 1.0)])
    for g in range(LEAVES // 16):
        at = slice(g * 16, g * 16 + 16)
        stack = jnp.concatenate([x[at], y[at], z[at], hi[at], mid[at], lo[at], one, zero], axis=0)
        feat = dot(stack, layout, ((0,), (0,)))
        for j in range(8):
            lhs_ref[g * 8 + j] = feat[:, j * 32:j * 32 + 32].astype(BF16)
    s = slot[...]
    base = jnp.int32(0)
    place = s
    for k in range(PEERS):
        here = (s >= k * CAPM) & (s < (k + 1) * CAPM)
        count_k = jnp.max(jnp.where(here, s - (k * CAPM - 1), 0))
        base_ref[k] = base
        place = jnp.where(here, s + (base - k * CAPM), place)
        base = base + ((count_k + 15) & -16)
    base_ref[PEERS] = base
    row = ((place >> 9) << 8) + (place & 255)
    power = jnp.where(row >= 512, 16.0, 1.0) * jnp.where((row & 256) > 0, 4.0, 1.0) * jnp.where((row & 128) > 0, 2.0, 1.0)
    code = (1.0 + (row & 127).astype(F32) * (1.0 / 128.0)) * power
    code = jnp.where((place & 256) > 0, -code, code)
    code = jnp.where(s >= 0, code, 0.0)
    dead = jnp.zeros((1, LEAVES), F32)
    last = (CHUNKS - 1) * CHUNK
    code = jnp.concatenate([code[:last], dead, code[last:], jnp.zeros((LANES - CHUNKS * CHUNK, LEAVES), F32)], axis=0)
    code_ref[...] = code.T


def prep(planes, count_row, far_slots, pair_slots, own):
    return pl.pallas_call(
        prep_kernel,
        out_shape=[
            jax.ShapeDtypeStruct((LEAVES // 2, LANES, 32), BF16), jax.ShapeDtypeStruct((8, LEAVES), I32),
            jax.ShapeDtypeStruct((LEAVES, LANES), F32), jax.ShapeDtypeStruct((16,), I32),
            jax.ShapeDtypeStruct((COLUMNS + 1, LEAVES), I32), jax.ShapeDtypeStruct(own.shape, BF16),
        ],
        in_specs=[HBM] * 5,
        out_specs=[VM, VM, VM, SM, VM, VM],
        scratch_shapes=[
            pltpu.VMEM((3, LEAVES, LANES), BF16), pltpu.VMEM((1, LEAVES), I32), pltpu.VMEM((OPS, LEAVES), I32),
            pltpu.VMEM((COLUMNS, LEAVES), I32), pltpu.SemaphoreType.DMA((5,)),
        ],
        compiler_params=params(24),
        name="prep",
    )(planes, count_row, far_slots, pair_slots, own)


def near_kernel(order, slot, lhs_ref, *refs):
    got = refs[:PEERS]
    out_ref, w_ref, q_ref = refs[PEERS:]
    one = jnp.ones((16, LANES), BF16)
    zero = jnp.zeros((16, LANES), BF16)
    layout = spread(False, -2.0, [(0, 1.0), (1, 1.0), (2, 1.0), (3, 1.0), (4, 1.0), (5, 1.0), (6, 1.0), (6, 1.0), (6, 1.0)])
    for k in range(PEERS):
        x, y, z, q = [got[k][c * CAP:(c + 1) * CAP, :] for c in range(4)]
        hi, mid, lo = squares(x, y, z, 0.09)
        q_ref[k * CAP:(k + 1) * CAP, :] = q.astype(F32)
        for g in range(CAP // 16):
            at = slice(g * 16, g * 16 + 16)
            stack = jnp.concatenate([x[at], y[at], z[at], hi[at], mid[at], lo[at], one, zero], axis=0)
            w_ref[k * CAP + g * 16:k * CAP + g * 16 + 16] = dot(layout, stack).astype(BF16).reshape(16, 16, LANES)
    w_ref[SLOTS] = one
    q_ref[SLOTS:SLOTS + 8, :] = jnp.zeros((8, LANES), F32)
    lane_row = iota((1, LANES), 1)
    group = 16

    def pair(p, rows):
        tiles, charge, leaf = [], [], []
        for a in range(2):
            leaf.append(order[0, 2 * p + a])
            for n in range(COLUMNS):
                s = slot[n, leaf[a]]
                t = w_ref[s]
                tiles.append(jnp.concatenate([t, zero] if a == 0 else [zero, t], axis=0))
                charge.append(q_ref[pl.ds(s, 1), :])
        lhs = lhs_ref[p][:rows]
        acc = [None, None]
        for i in range(0, 2 * COLUMNS, 2):
            inv = lax.rsqrt(dot(lhs, jnp.concatenate(tiles[i:i + 2], axis=1)))
            for j in (i, i + 1):
                a = j // COLUMNS
                term = inv[:, (j - i) * LANES:(j - i + 1) * LANES] * charge[j]
                acc[a] = term if acc[a] is None else acc[a] + term
        for a in range(2):
            full = acc[a]
            if rows < LANES:
                full = jnp.concatenate([full, jnp.zeros((LANES - rows, LANES), F32)], axis=0)
            row = jnp.sum(full.T, axis=0, keepdims=True)
            out_ref[pl.ds(leaf[a], 1), :] = jnp.where(lane_row < slot[COLUMNS, leaf[a]], row, 0.0)

    def body(g, _):
        most = slot[COLUMNS, order[0, g * group]]
        for rows in range(STEP, LANES + 1, STEP):
            @pl.when((most > rows - STEP) & (most <= rows))
            def _():
                for p in range(group // 2):
                    pair(g * (group // 2) + p, rows)
        return 0

    lax.fori_loop(0, LEAVES // group, body, 0)


STEP = 32


def near(order, pair, lhs, got):
    return pl.pallas_call(
        near_kernel,
        out_shape=jax.ShapeDtypeStruct((LEAVES, LANES), F32),
        in_specs=[SM] * 2 + [VM] * (1 + PEERS),
        out_specs=VM,
        scratch_shapes=[
            pltpu.VMEM((SLOTS + 1, 16, LANES), BF16), pltpu.VMEM((SLOTS + 8, LANES), F32),
        ],
        compiler_params=params(24),
        name="near",
    )(order, pair, lhs, *got)


def far_kernel(tile_ref, base_ref, code_ref, m2l_h, near_ref, *refs):
    got = refs[:PEERS]
    part_refs = refs[PEERS:PEERS + 4]
    local, table, whole, m2l, sems = refs[PEERS + 4:]
    copies = fetch([(m2l_h, m2l)], sems)
    table[...] = jnp.zeros_like(table)
    for k in range(PEERS):
        for b in range(CAPM // 16):
            at = base_ref[k] + 16 * b
            row = pl.multiple_of(((at >> 9) << 8) + (at & 255), 16)
            table[(at >> 8) & 1, pl.ds(row, 16), :] = got[k][4 * CAP + 16 * b:4 * CAP + 16 * b + 16, :]
    local[...] = jnp.zeros_like(local)
    whole[:, :LANES] = table[0]
    whole[:, LANES:] = table[1]
    lane = iota((1, LANES), 1).astype(F32) * (1.0 / 128.0) + 1.0

    def run(depth):
        marks = [jnp.broadcast_to((lane * (2.0 ** j)).astype(BF16), (LEAVES, LANES)) for j in range(depth // LANES)]

        def body(c, _):
            code = pltpu.roll(code_ref[...], lax.rem(LANES - c * CHUNK, LANES), 1)[:, :CHUNK]
            weights = whole[:depth]
            mats = m2l[pl.ds(jnp.minimum(c * CHUNK, OPS - CHUNK), CHUNK)].reshape(CHUNK * LANES, LANES)
            rows = []
            for i in range(CHUNK):
                col = jnp.broadcast_to(code[:, i:i + 1], (LEAVES, LANES))
                wide = jnp.abs(col.astype(BF16))
                hot = jnp.concatenate([jnp.where(wide == m, jnp.ones_like(wide), jnp.zeros_like(wide)) for m in marks], axis=1)
                both = dot(hot, weights)
                rows.append(jnp.where(col < 0.0, both[:, LANES:], both[:, :LANES]).astype(BF16))
            total = local[...]
            for i in range(0, CHUNK, 8):
                total = total + dot(jnp.concatenate(rows[i:i + 8], axis=1), mats[i * LANES:(i + 8) * LANES])
            local[...] = total
            return 0

        lax.fori_loop(0, CHUNKS, body, 0)

    for c in copies:
        c.wait()
    small = base_ref[PEERS] <= 1536

    @pl.when(small)
    def _():
        run(768)

    @pl.when(jnp.logical_not(small))
    def _():
        run(1024)

    rows = LEAVES // 4
    for d in range(4):
        at = pl.multiple_of(lax.rem(tile_ref[0] + d, 4) * rows, rows)
        part_refs[d][:, :LANES] = near_ref[pl.ds(at, rows), :]
        part_refs[d][:, LANES:] = local[pl.ds(at, rows), :]


def far(tile, base, code, m2l, near_part, got):
    return pl.pallas_call(
        far_kernel,
        out_shape=[jax.ShapeDtypeStruct((LEAVES // 4, 2 * LANES), F32)] * 4,
        in_specs=[SM, SM, VM, HBM, VM] + [VM] * PEERS,
        out_specs=[VM] * 4,
        scratch_shapes=[
            pltpu.VMEM((LEAVES, LANES), F32), pltpu.VMEM((2, TABLE, LANES), BF16),
            pltpu.VMEM((TABLE, 2 * LANES), BF16),
            pltpu.VMEM((OPS, LANES, LANES), BF16), pltpu.SemaphoreType.DMA((1,)),
        ],
        compiler_params=params(32),
        name="far",
    )(tile, base, code, m2l, near_part, *got)


def per_device(positions, charges, leaf_counts, multipoles, m2l_ops, leaf_send, pair_slots, far_send, far_slots):
    reach = (PEERS - 1) // 2
    slabs = lax.axis_size("slab")
    tiles = lax.axis_size("tile")
    planes = jnp.transpose(positions, (1, 0, 2))
    count_row = leaf_counts.reshape(1, LEAVES)
    payload = pack(planes, charges, count_row, multipoles, leaf_send, far_send)
    got = list(payload)
    for step in range(reach, 0, -1):
        for k in (reach + step, reach - step):
            hops = k - reach
            got[k] = lax.ppermute(payload[k], "slab", [(s, (s + hops) % slabs) for s in range(slabs)])
    lhs, order, code, base, pair, got[reach] = prep(planes, count_row, far_slots.T, pair_slots.T, payload[reach])
    near_part = near(order, pair, lhs, got)
    tile = lax.axis_index("tile").astype(I32).reshape(1)
    parts = far(tile, base, code, m2l_ops, near_part, got)
    total = parts[0]
    for step in range(1, tiles):
        total = total + lax.ppermute(parts[step], "tile", [(t, (t + step) % tiles) for t in range(tiles)])
    return total[:, :LANES], total[:, LANES:]


def solution(mesh):
    return jax.shard_map(
        per_device,
        mesh=mesh,
        in_specs=(
            P("slab", None, None),
            P("slab", None),
            P("slab"),
            P("slab", None),
            P("tile", None, None),
            P("slab", "tile"),
            P("slab", "tile"),
            P("slab", "tile"),
            P("slab", "tile"),
        ),
        out_specs=(P(("slab", "tile"), None), P(("slab", "tile"), None)),
        check_vma=False,
    )
```

time: 267 us -> 75.8 us (0.28); the launches traced: 263 us -> 74.7 us
  local copies, waits for them, and re-layouts: 99.7 us -> 4.72 us
  other arithmetic: 66.1 us -> 0.02 us
  starting transfers between devices: 51.7 us -> 14.2 us
  Pallas kernels: 0 us -> 37.4 us
  between operations: 14.5 us -> 0.73 us
  waiting for transfers between devices: 24.7 us -> 17.6 us
  matrix products: 4.66 us -> 0 us
    reduce_sum x16 -> x0, other arithmetic: 62.8 us -> none  [pair_block(): return jnp.sum(inverse * source_q[:, :, None, :], axis=(1, 3))]
    gather x4 -> x0, local copies, waits for them, and re-layouts: 54.8 us -> none  [the longest x1 41.2 us: per_device(): far_flat[far_index.reshape(-1)].reshape(slab_leaves, op_count * coef_count)]
    pallas_call x0 -> x4, Pallas kernels: none -> 37.4 us  [the longest x1 17.6 us: near(): pl.pallas_call(near_kernel, out_shape=jax.ShapeDtypeStruct((LEAVES, LANES...]
    ppermute x16 -> x11, starting transfers between devices: 51.6 us -> 14.2 us  [the longest x8 10.7 us: per_device(): lax.ppermute(payload[k], 'slab', [(s, (s + hops) % slabs) for s in range(...]
    reduce_scatter x2 -> x0, waiting for transfers between devices: 24.6 us -> none  [the longest x1 24.6 us: per_device(): lax.psum_scatter(near, 'tile', scatter_dimension=0, tiled=True)]
    ppermute x16 -> x11, waiting for transfers between devices: 0.04 us -> 17.6 us  [the longest x8 12 us: per_device(): lax.ppermute(payload[k], 'slab', [(s, (s + hops) % slabs) for s in range(...]
    dynamic_slice x32 -> x0, local copies, waits for them, and re-layouts: 15.4 us -> none  [near_field(): lax.map(pair_block, (targets.reshape((block_count, block_leaves) + target...]
    reshape x2 -> x0, local copies, waits for them, and re-layouts: 9.88 us -> none  [the longest x1 9.62 us: per_device(): far_flat[far_index.reshape(-1)].reshape(slab_leaves, op_count * coef_count)]
  transfers between devices with their start and end apart: 18 -> 11, of which waited for: 1 -> 7; matrix products, arithmetic and copies ran while one was open for 62% -> 0% of each run, Pallas kernels for 0% -> 5%
where the time goes in v2:
time: 75.8 us; the launch traced here: 74.7 us
  Pallas kernels  37.4 us (49%)
  waiting for transfers between devices  17.6 us (23%)
  starting transfers between devices  14.2 us (19%)
  local copies, waits for them, and re-layouts  4.72 us (6%)
    pallas_call x1, Pallas kernels, near(): pl.pallas_call(near_kernel, out_shape=jax.ShapeDtypeStruct((LEAVES, LANES...  17.6 us
    pallas_call x1, Pallas kernels, far(): pl.pallas_call(far_kernel, out_shape=[jax.ShapeDtypeStruct((LEAVES // 4,...  13.1 us
    ppermute x8, waiting for transfers between devices, per_device(): lax.ppermute(payload[k], 'slab', [(s, (s + hops) % slabs) for s in range(...  12 us
    ppermute x8, starting transfers between devices, per_device(): lax.ppermute(payload[k], 'slab', [(s, (s + hops) % slabs) for s in range(...  10.7 us
    ppermute x3, waiting for transfers between devices, per_device(): lax.ppermute(parts[step], 'tile', [(t, (t + step) % tiles) for t in range...  5.6 us
    unnamed x12, local copies, waits for them, and re-layouts  4.09 us
    pallas_call x1, Pallas kernels, prep(): pl.pallas_call(prep_kernel, out_shape=[jax.ShapeDtypeStruct((LEAVES // 2,...  4.01 us
    ppermute x3, starting transfers between devices, per_device(): lax.ppermute(parts[step], 'tile', [(t, (t + step) % tiles) for t in range...  3.48 us
  transfers between devices with their start and end apart: 11, of which 7 were waited for; matrix products, arithmetic and copies ran while one was open for 0% of the time, Pallas kernels for 5%

profile of v2, /device:TPU:6, one launch (start us, length us, event | category | flops | bytes accessed | tf_op | source)
XLA Modules:
  0.0 74.7 jit_solution(15588928841570708430)
XLA Ops:
  0.6 0.0 copy-start
  0.6 2.8 %pack.1 = (bf16[448,128]{1,0:T(8,128)(2,1)}, bf16[448,128]{1,0:T(8,128)(2,1)}, bf16[448,128]{1,0:T(8,128)(2,1)}, bf16[448,128]{1,0:T(8,128)(2,1)}, bf16[448,128]...) custom-call(bf16[3,256,128]{2,1,0:T(8,128)(2,1)} %bitcast.5, ...), custom_call_target="tpu_custom_call" | custom-call | tf_op jit(solution)/shard_map/pack/pallas_call | solution.py:67
  3.4 8.8 %collective-permute-start = (bf16[448,128]{1,0:T(8,128)(2,1)}, bf16[448,128]{1,0:T(8,128)(2,1)S(1)}, u32[]{:S(2)}, u32[]{:S(2)}) collective-permute-start(bf16[448,128]{1,0:T(8,128)(2,1)} %get-tuple-element.27), channel_id=1, source_target_pairs={{0,240},{4,244},{8,248},{12,252},{16,0},{20,4},{24,8},{28,12},{32,... | collective-permute-start | bytes 344072 | tf_op jit(solution)/shard_map/ppermute | solution.py:321
  12.2 0.6 collective-permute-start.1
  12.8 0.4 collective-permute-start.2
  13.3 0.7 collective-permute-start.3
  14.0 0.1 collective-permute-start.4
  14.1 4.0 %collective-permute-done.refs_0_ = bf16[448,128]{1,0:T(8,128)(2,1)S(1)} collective-permute-done((bf16[448,128]{1,0:T(8,128)(2,1)}, bf16[448,128]{1,0:T(8,128)(2,1)S(1)}, u32[]{:S(2)}, u32[]{:S(2)}) %collective-permute-start) | collective-permute-done | bytes 114720 | tf_op jit(solution)/shard_map/ppermute | solution.py:321
  18.1 0.0 collective-permute-start.5
  18.1 3.5 %collective-permute-done.1.refs_1_ = bf16[448,128]{1,0:T(8,128)(2,1)S(1)} collective-permute-done((bf16[448,128]{1,0:T(8,128)(2,1)}, bf16[448,128]{1,0:T(8,128)(2,1)S(1)}, u32[]{:S(2)}, u32[]{:S(2)}) %collective-permute-start.1) | collective-permute-done | bytes 114720 | tf_op jit(solution)/shard_map/ppermute | solution.py:321
  21.7 0.0 collective-permute-start.6
  21.7 1.9 %collective-permute-done.2.refs_2_ = bf16[448,128]{1,0:T(8,128)(2,1)S(1)} collective-permute-done((bf16[448,128]{1,0:T(8,128)(2,1)}, bf16[448,128]{1,0:T(8,128)(2,1)S(1)}, u32[]{:S(2)}, u32[]{:S(2)}) %collective-permute-start.2) | collective-permute-done | bytes 114720 | tf_op jit(solution)/shard_map/ppermute | solution.py:321
  23.6 0.0 collective-permute-start.7
  23.6 0.0 copy-start.1
  23.6 0.9 %copy-done.1 = bf16[256,3,128]{2,0,1:T(8,128)(2,1)S(1)} copy-done((bf16[256,3,128]{2,0,1:T(8,128)(2,1)S(1)}, bf16[256,3,128]{2,0,1:T(8,128)(2,1)}, u32[]{:S(2)}) %copy-start.1) | copy-done | bytes 196632
  24.5 0.0 copy-start.2
  24.5 0.9 %copy-done.2 = bf16[448,128]{1,0:T(8,128)(2,1)S(1)} copy-done((bf16[448,128]{1,0:T(8,128)(2,1)S(1)}, bf16[448,128]{1,0:T(8,128)(2,1)}, u32[]{:S(2)}) %copy-start.2) | copy-done | bytes 114712
  25.4 0.0 copy-start.3
  25.4 0.9 %copy-done.3 = s32[256,79]{0,1:T(8,128)S(1)} copy-done((s32[256,79]{0,1:T(8,128)S(1)}, s32[256,79]{0,1:T(8,128)}, u32[]{:S(2)}) %copy-start.3) | copy-done | bytes 80920
  26.3 0.0 copy-start.4
  26.3 0.7 copy-done.4
  27.0 0.0 copy-start.5
  27.0 0.7 copy-done.5
  27.7 4.0 %prep.1 = (bf16[128,128,32]{2,1,0:T(8,128)(2,1)S(1)}, s32[8,256]{1,0:T(8,128)S(1)}, f32[256,128]{1,0:T(8,128)S(1)}, s32[16]{0:T(128)S(1)}, s32[8,256]{1,0:T(8,128)S(1)}, /*index=5*/bf16[448,128]{1,0:T(8,128)(2,1)S(1)}) custom-call(bf16[3,256,128]{2,1,0:T(8,128)(2,1)S(1)} %bitcast.6, s32[1,256]{1,0:T(1,128)S(1)} %bitcast.10, s32[79,256]{1,0:T(8,128)S(1)} %bitcast.7, ...), custom_call_target="tpu_custom_call" | custom-call | tf_op jit(solution)/shard_map/prep/pallas_call | solution.py:147
  31.7 0.0 collective-permute-done.3.refs_3_
  31.7 0.0 collective-permute-done.4.refs_5_
  31.7 0.0 collective-permute-done.5.refs_6_
  31.7 0.0 collective-permute-done.6.refs_7_
  31.7 2.5 %collective-permute-done.7.refs_8_ = bf16[448,128]{1,0:T(8,128)(2,1)S(1)} collective-permute-done((bf16[448,128]{1,0:T(8,128)(2,1)}, bf16[448,128]{1,0:T(8,128)(2,1)S(1)}, u32[]{:S(2)}, u32[]{:S(2)}) %collective-permute-start.7) | collective-permute-done | bytes 114720 | tf_op jit(solution)/shard_map/ppermute | solution.py:321
  34.2 17.6 %near.1.near_ref = f32[256,128]{1,0:T(8,128)S(1)} custom-call(s32[8,256]{1,0:T(8,128)S(1)} %get-tuple-element.24.order, s32[8,256]{1,0:T(8,128)S(1)} %get-tuple-element.25.slot, bf16[128,128,32]{2,1,0:T(8,128)(2,1)S(1)} %get-tuple-element.26.lhs_ref, bf16[448,128]{1,0:T(8,128)(2,1)S(1)} %collective-permute-done.refs_0_, ...), custom_call_target="tpu_custom_call" | custom-call | tf_op jit(solution)/shard_map/near/pallas_call | solution.py:224
  51.9 0.0 copy-done
  51.9 13.1 %far.1 = (f32[64,256]{1,0:T(8,128)S(1)}, f32[64,256]{1,0:T(8,128)S(1)}, f32[64,256]{1,0:T(8,128)S(1)}, f32[64,256]{1,0:T(8,128)S(1)}) custom-call(s32[1]{0:T(128)} %bitcast.tile_ref, s32[16]{0:T(128)S(1)} %get-tuple-element.22.base_ref, f32[256,128]{1,0:T(8,128)S(1)} %get-tuple-element.23.code_ref, bf16[79,128,128]{2,1,0:T(8,128)(2,1)S(1)} %copy-done, ...), custom_call_target="tpu_custom_call" | custom-call | tf_op jit(solution)/shard_map/far/pallas_call | solution.py:295
  64.9 0.9 %collective-permute-start.10 = (f32[64,256]{1,0:T(8,128)S(1)}, f32[64,256]{1,0:T(8,128)S(1)}, u32[]{:S(2)}, u32[]{:S(2)}) collective-permute-start(f32[64,256]{1,0:T(8,128)S(1)} %get-tuple-element.39), channel_id=1, source_target_pairs={{0,3},{1,0},{2,1},{3,2},{4,7},{5,4},{6,5},{7,6},{8,11},{9,8},{10,9... | collective-permute-start | bytes 196616 | tf_op jit(solution)/shard_map/ppermute | solution.py:328
  65.8 2.4 %collective-permute-start.8 = (f32[64,256]{1,0:T(8,128)S(1)}, f32[64,256]{1,0:T(8,128)S(1)}, u32[]{:S(2)}, u32[]{:S(2)}) collective-permute-start(f32[64,256]{1,0:T(8,128)S(1)} %get-tuple-element.37), channel_id=1, source_target_pairs={{0,1},{1,2},{2,3},{3,0},{4,5},{5,6},{6,7},{7,4},{8,9},{9,10},{10,1... | collective-permute-start | bytes 196616 | tf_op jit(solution)/shard_map/ppermute | solution.py:328
  68.2 0.2 collective-permute-start.9
  68.4 2.1 %collective-permute-done.10 = f32[64,256]{1,0:T(8,128)S(1)} collective-permute-done((f32[64,256]{1,0:T(8,128)S(1)}, f32[64,256]{1,0:T(8,128)S(1)}, u32[]{:S(2)}, u32[]{:S(2)}) %collective-permute-start.10) | collective-permute-done | bytes 65568 | tf_op jit(solution)/shard_map/ppermute | solution.py:328
  70.5 0.5 collective-permute-done.8
  71.0 3.0 %collective-permute-done.9 = f32[64,256]{1,0:T(8,128)S(1)} collective-permute-done((f32[64,256]{1,0:T(8,128)S(1)}, f32[64,256]{1,0:T(8,128)S(1)}, u32[]{:S(2)}, u32[]{:S(2)}) %collective-permute-start.9) | collective-permute-done | bytes 65568 | tf_op jit(solution)/shard_map/ppermute | solution.py:328
  74.0 0.6 fusion
  (1 shorter events, 0.0 us)
Async XLA Ops:
  0.6 51.2 %copy-start = (bf16[79,128,128]{2,1,0:T(8,128)(2,1)S(1)}, bf16[79,128,128]{2,1,0:T(8,128)(2,1)}, u32[]{:S(2)}) copy-start(bf16[79,128,128]{2,1,0:T(8,128)(2,1)} %m2l_h.1) | copy-start | bytes 7766020
  3.4 14.7 %collective-permute-start = (bf16[448,128]{1,0:T(8,128)(2,1)}, bf16[448,128]{1,0:T(8,128)(2,1)S(1)}, u32[]{:S(2)}, u32[]{:S(2)}) collective-permute-start(bf16[448,128]{1,0:T(8,128)(2,1)} %get-tuple-element.27), channel_id=1, source_target_pairs={{0,240},{4,244},{8,248},{12,252},{16,0},{20,4},{24,8},{28,12},{32,... | collective-permute-start | bytes 344072 | tf_op jit(solution)/shard_map/ppermute | solution.py:321
  12.2 9.4 %collective-permute-start.1 = (bf16[448,128]{1,0:T(8,128)(2,1)}, bf16[448,128]{1,0:T(8,128)(2,1)S(1)}, u32[]{:S(2)}, u32[]{:S(2)}) collective-permute-start(bf16[448,128]{1,0:T(8,128)(2,1)} %get-tuple-element.28), channel_id=1, source_target_pairs={{0,244},{4,248},{8,252},{12,0},{16,4},{20,8},{24,12},{28,16},{32,2... | collective-permute-start | bytes 344072 | tf_op jit(solution)/shard_map/ppermute | solution.py:321
  12.8 10.7 %collective-permute-start.2 = (bf16[448,128]{1,0:T(8,128)(2,1)}, bf16[448,128]{1,0:T(8,128)(2,1)S(1)}, u32[]{:S(2)}, u32[]{:S(2)}) collective-permute-start(bf16[448,128]{1,0:T(8,128)(2,1)} %get-tuple-element.29), channel_id=1, source_target_pairs={{0,248},{4,252},{8,0},{12,4},{16,8},{20,12},{24,16},{28,20},{32,24... | collective-permute-start | bytes 344072 | tf_op jit(solution)/shard_map/ppermute | solution.py:321
  13.3 18.4 %collective-permute-start.3 = (bf16[448,128]{1,0:T(8,128)(2,1)}, bf16[448,128]{1,0:T(8,128)(2,1)S(1)}, u32[]{:S(2)}, u32[]{:S(2)}) collective-permute-start(bf16[448,128]{1,0:T(8,128)(2,1)} %get-tuple-element.30), channel_id=1, source_target_pairs={{0,252},{4,0},{8,4},{12,8},{16,12},{20,16},{24,20},{28,24},{32,28}... | collective-permute-start | bytes 344072 | tf_op jit(solution)/shard_map/ppermute | solution.py:321
  14.0 17.7 %collective-permute-start.4 = (bf16[448,128]{1,0:T(8,128)(2,1)}, bf16[448,128]{1,0:T(8,128)(2,1)S(1)}, u32[]{:S(2)}, u32[]{:S(2)}) collective-permute-start(bf16[448,128]{1,0:T(8,128)(2,1)} %get-tuple-element.32), channel_id=1, source_target_pairs={{0,4},{4,8},{8,12},{12,16},{16,20},{20,24},{24,28},{28,32},{32,36}... | collective-permute-start | bytes 344072 | tf_op jit(solution)/shard_map/ppermute | solution.py:321
  18.1 13.6 %collective-permute-start.5 = (bf16[448,128]{1,0:T(8,128)(2,1)}, bf16[448,128]{1,0:T(8,128)(2,1)S(1)}, u32[]{:S(2)}, u32[]{:S(2)}) collective-permute-start(bf16[448,128]{1,0:T(8,128)(2,1)} %get-tuple-element.33), channel_id=1, source_target_pairs={{0,8},{4,12},{8,16},{12,20},{16,24},{20,28},{24,32},{28,36},{32,40... | collective-permute-start | bytes 344072 | tf_op jit(solution)/shard_map/ppermute | solution.py:321
  21.7 10.0 %collective-permute-start.6 = (bf16[448,128]{1,0:T(8,128)(2,1)}, bf16[448,128]{1,0:T(8,128)(2,1)S(1)}, u32[]{:S(2)}, u32[]{:S(2)}) collective-permute-start(bf16[448,128]{1,0:T(8,128)(2,1)} %get-tuple-element.34), channel_id=1, source_target_pairs={{0,12},{4,16},{8,20},{12,24},{16,28},{20,32},{24,36},{28,40},{32,4... | collective-permute-start | bytes 344072 | tf_op jit(solution)/shard_map/ppermute | solution.py:321
  23.6 10.7 %collective-permute-start.7 = (bf16[448,128]{1,0:T(8,128)(2,1)}, bf16[448,128]{1,0:T(8,128)(2,1)S(1)}, u32[]{:S(2)}, u32[]{:S(2)}) collective-permute-start(bf16[448,128]{1,0:T(8,128)(2,1)} %get-tuple-element.35), channel_id=1, source_target_pairs={{0,16},{4,20},{8,24},{12,28},{16,32},{20,36},{24,40},{28,44},{32,4... | collective-permute-start | bytes 344072 | tf_op jit(solution)/shard_map/ppermute | solution.py:321
  23.6 0.9 %copy-start.1 = (bf16[256,3,128]{2,0,1:T(8,128)(2,1)S(1)}, bf16[256,3,128]{2,0,1:T(8,128)(2,1)}, u32[]{:S(2)}) copy-start(bf16[256,3,128]{2,0,1:T(8,128)(2,1)} %param.9) | copy-start | bytes 589828
  24.5 0.9 %copy-start.2 = (bf16[448,128]{1,0:T(8,128)(2,1)S(1)}, bf16[448,128]{1,0:T(8,128)(2,1)}, u32[]{:S(2)}) copy-start(bf16[448,128]{1,0:T(8,128)(2,1)} %get-tuple-element.21.own_h) | copy-start | bytes 344068
  25.4 0.9 %copy-start.3 = (s32[256,79]{0,1:T(8,128)S(1)}, s32[256,79]{0,1:T(8,128)}, u32[]{:S(2)}) copy-start(s32[256,79]{0,1:T(8,128)} %param.17) | copy-start | bytes 242692
  26.3 0.7 copy-start.4
  27.0 0.7 copy-start.5
  64.9 5.6 %collective-permute-start.10 = (f32[64,256]{1,0:T(8,128)S(1)}, f32[64,256]{1,0:T(8,128)S(1)}, u32[]{:S(2)}, u32[]{:S(2)}) collective-permute-start(f32[64,256]{1,0:T(8,128)S(1)} %get-tuple-element.39), channel_id=1, source_target_pairs={{0,3},{1,0},{2,1},{3,2},{4,7},{5,4},{6,5},{7,6},{8,11},{9,8},{10,9... | collective-permute-start | bytes 196616 | tf_op jit(solution)/shard_map/ppermute | solution.py:328
  65.8 5.2 %collective-permute-start.8 = (f32[64,256]{1,0:T(8,128)S(1)}, f32[64,256]{1,0:T(8,128)S(1)}, u32[]{:S(2)}, u32[]{:S(2)}) collective-permute-start(f32[64,256]{1,0:T(8,128)S(1)} %get-tuple-element.37), channel_id=1, source_target_pairs={{0,1},{1,2},{2,3},{3,0},{4,5},{5,6},{6,7},{7,4},{8,9},{9,10},{10,1... | collective-permute-start | bytes 196616 | tf_op jit(solution)/shard_map/ppermute | solution.py:328
  68.2 5.8 %collective-permute-start.9 = (f32[64,256]{1,0:T(8,128)S(1)}, f32[64,256]{1,0:T(8,128)S(1)}, u32[]{:S(2)}, u32[]{:S(2)}) collective-permute-start(f32[64,256]{1,0:T(8,128)S(1)} %get-tuple-element.38), channel_id=1, source_target_pairs={{0,2},{1,3},{2,0},{3,1},{4,6},{5,7},{6,4},{7,5},{8,10},{9,11},{10,... | collective-permute-start | bytes 196616 | tf_op jit(solution)/shard_map/ppermute | solution.py:328

commit v3 on v2

--- a/solution.py
+++ b/solution.py
@@ -12,8 +12,9 @@
 LEAVES, LANES = 256, 128
 COLUMNS, OPS = 7, 79
 SLOTS = PEERS * CAP
-CHUNK = 16
-CHUNKS = 5
+PAYLOAD = 4 * CAP + CAPM
+CHUNK = 40
+CHUNKS = 2
 TABLE = 1024
 HBM = pl.BlockSpec(memory_space=pltpu.HBM)
 VM = pl.BlockSpec(memory_space=pltpu.VMEM)
@@ -43,10 +44,30 @@
     return jnp.broadcast_to(row.astype(F32), (8, LEAVES)).T[:, 0:1]
 
 
-def pack_kernel(pos_h, charge_h, count_h, multi_h, leaf_h, far_h, *refs):
+def routes():
+    reach = (PEERS - 1) // 2
+    pairs = [(reach, reach)]
+    for step in range(reach, 0, -1):
+        pairs += [(reach - step, reach + step), (reach + step, reach - step)]
+    return pairs
+
+
+def arrived(odd, got, k, part):
+    reach = (PEERS - 1) // 2
+    if k == reach:
+        return got[0][part]
+    step = abs(k - reach)
+    first = 1 + 2 * (reach - step)
+    upward = odd == step % 2
+    a, b = (first, first + 1) if k > reach else (first + 1, first)
+    return jnp.where(upward, got[a][part], got[b][part])
+
+
+def pack_kernel(odd_ref, pos_h, charge_h, count_h, multi_h, leaf_h, far_h, slot_h, pair_h, *refs):
     out_refs = refs[:PEERS]
-    pos, charge, count, multi_ref, leaf, far_s, sems = refs[PEERS:]
-    for c in fetch([(pos_h, pos), (charge_h, charge), (count_h, count), (multi_h, multi_ref), (leaf_h, leaf), (far_h, far_s)], sems):
+    ints_ref = refs[PEERS]
+    pos, charge, count, multi_ref, leaf, far_s, slot, pair, sems = refs[PEERS + 1:]
+    for c in fetch([(pos_h, pos), (charge_h, charge), (count_h, count), (multi_h, multi_ref), (leaf_h, leaf), (far_h, far_s), (slot_h, slot), (pair_h, pair)], sems):
         c.wait()
     live = iota((LEAVES, LANES), 1).astype(F32) < column(count[...])
     masked = jnp.where(live, charge[...].astype(F32), 0.0).astype(BF16)
@@ -54,29 +75,39 @@
     box = iota((LEAVES, CAP), 0)
     boxm = iota((LEAVES, CAPM), 0)
     multi = multi_ref[...]
-    for k in range(PEERS):
-        pick = jnp.where(box == leaf[k:k + 1, :], 1.0, 0.0).astype(BF16)
+    even = odd_ref[0] == 0
+    for i, (low, high) in enumerate(routes()):
+        leaf_row = jnp.where(even, leaf[high:high + 1, :], leaf[low:low + 1, :])
+        far_row = jnp.where(even, far_s[high:high + 1, :], far_s[low:low + 1, :])
+        pick = jnp.where(box == leaf_row, 1.0, 0.0).astype(BF16)
         rows = dot(pick, table, ((0,), (0,))).astype(BF16)
         for c in range(4):
-            out_refs[k][c * CAP:(c + 1) * CAP, :] = rows[:, c * LANES:(c + 1) * LANES]
-        pickm = jnp.where(boxm == far_s[k:k + 1, :], 1.0, 0.0).astype(BF16)
-        out_refs[k][4 * CAP:4 * CAP + CAPM, :] = dot(pickm, multi, ((0,), (0,))).astype(BF16)
-
-
-def pack(planes, charges, count_row, multi, leaf_send, far_send):
+            out_refs[i][c * CAP:(c + 1) * CAP, :] = rows[:, c * LANES:(c + 1) * LANES]
+        pickm = jnp.where(boxm == far_row, 1.0, 0.0).astype(BF16)
+        out_refs[i][4 * CAP:4 * CAP + CAPM, :] = dot(pickm, multi, ((0,), (0,))).astype(BF16)
+    for c in range(3):
+        out_refs[0][PAYLOAD + c * LEAVES:PAYLOAD + (c + 1) * LEAVES, :] = pos[c]
+    ints_ref[...] = jnp.zeros_like(ints_ref)
+    ints_ref[0:OPS, :] = slot[...]
+    ints_ref[80:80 + COLUMNS, :] = pair[...]
+    ints_ref[88:89, :] = count[...]
+
+
+def pack(odd, planes, charges, count_row, multi, leaf_send, far_send, far_slots, pair_slots):
     return pl.pallas_call(
         pack_kernel,
-        out_shape=[jax.ShapeDtypeStruct((4 * CAP + CAPM, LANES), BF16)] * PEERS,
-        in_specs=[HBM] * 6,
-        out_specs=[VM] * PEERS,
+        out_shape=[jax.ShapeDtypeStruct((PAYLOAD + 3 * LEAVES, LANES), BF16)]
+        + [jax.ShapeDtypeStruct((PAYLOAD, LANES), BF16)] * (PEERS - 1) + [jax.ShapeDtypeStruct((96, LEAVES), I32)],
+        in_specs=[SM] + [HBM] * 8,
+        out_specs=[VM] * (PEERS + 1),
         scratch_shapes=[
             pltpu.VMEM((3, LEAVES, LANES), BF16), pltpu.VMEM((LEAVES, LANES), BF16), pltpu.VMEM((1, LEAVES), I32),
             pltpu.VMEM((LEAVES, LANES), BF16), pltpu.VMEM((PEERS, CAP), I32), pltpu.VMEM((PEERS, CAPM), I32),
-            pltpu.SemaphoreType.DMA((6,)),
+            pltpu.VMEM((OPS, LEAVES), I32), pltpu.VMEM((COLUMNS, LEAVES), I32), pltpu.SemaphoreType.DMA((8,)),
         ],
         compiler_params=params(56),
         name="pack",
-    )(planes, charges, count_row, multi, leaf_send, far_send)
+    )(odd, planes, charges, count_row, multi, leaf_send, far_send, far_slots, pair_slots)
 
 
 def squares(x, y, z, bias):
@@ -99,19 +130,19 @@
     return jnp.where(item == item2, value, 0.0).astype(BF16)
 
 
-def prep_kernel(pos_h, count_h, slot_h, pair_h, own_h, lhs_ref, order_ref, code_ref, base_ref, pair_ref, own_ref, pos, count, slot, pair, sems):
-    copies = fetch([(pos_h, pos), (count_h, count), (slot_h, slot), (pair_h, pair), (own_h, own_ref)], sems)
-    for c in copies:
-        c.wait()
+def prep_kernel(own_in_ref, ints_ref, lhs_ref, order_ref, code_ref, base_ref, pair_ref, own_ref):
+    own_ref[...] = own_in_ref[:PAYLOAD, :]
+    count = ints_ref[88:89, :]
+    pair = ints_ref[80:80 + COLUMNS, :]
     leaf_row = iota((1, LEAVES), 1).astype(F32)
-    key_row = count[...].astype(F32) * LEAVES + leaf_row
+    key_row = count.astype(F32) * LEAVES + leaf_row
     key_col = jnp.broadcast_to(key_row, (8, LEAVES)).T[:, 0:1]
     rank = jnp.sum(jnp.where(key_col > key_row, 1.0, 0.0), axis=0, keepdims=True)
     move = jnp.where(rank == iota((LEAVES, LEAVES), 0).astype(F32), 1.0, 0.0).astype(BF16)
     order_ref[...] = dot(jnp.broadcast_to(leaf_row, (8, LEAVES)).astype(BF16), move, ((1,), (1,))).astype(I32)
-    pair_ref[:COLUMNS, :] = jnp.where(pair[...] < 0, SLOTS, pair[...])
-    pair_ref[COLUMNS:, :] = count[...]
-    x, y, z = [dot(move, pos[c]).astype(BF16) for c in range(3)]
+    pair_ref[:COLUMNS, :] = jnp.where(pair < 0, SLOTS, pair)
+    pair_ref[COLUMNS:, :] = count
+    x, y, z = [dot(move, own_in_ref[PAYLOAD + c * LEAVES:PAYLOAD + (c + 1) * LEAVES, :]).astype(BF16) for c in range(3)]
     hi, mid, lo = squares(x, y, z, 0.0)
     one = jnp.ones((16, LANES), BF16)
     zero = jnp.zeros((16, LANES), BF16)
@@ -120,9 +151,9 @@
         at = slice(g * 16, g * 16 + 16)
         stack = jnp.concatenate([x[at], y[at], z[at], hi[at], mid[at], lo[at], one, zero], axis=0)
         feat = dot(stack, layout, ((0,), (0,)))
-        for j in range(8):
-            lhs_ref[g * 8 + j] = feat[:, j * 32:j * 32 + 32].astype(BF16)
-    s = slot[...]
+        lhs_ref[2 * g] = feat[:, :LANES].astype(BF16)
+        lhs_ref[2 * g + 1] = feat[:, LANES:].astype(BF16)
+    s = ints_ref[0:OPS, :]
     base = jnp.int32(0)
     place = s
     for k in range(PEERS):
@@ -143,33 +174,29 @@
     code_ref[...] = code.T
 
 
-def prep(planes, count_row, far_slots, pair_slots, own):
+def prep(own, ints):
     return pl.pallas_call(
         prep_kernel,
         out_shape=[
-            jax.ShapeDtypeStruct((LEAVES // 2, LANES, 32), BF16), jax.ShapeDtypeStruct((8, LEAVES), I32),
+            jax.ShapeDtypeStruct((LEAVES // 8, LANES, LANES), BF16), jax.ShapeDtypeStruct((8, LEAVES), I32),
             jax.ShapeDtypeStruct((LEAVES, LANES), F32), jax.ShapeDtypeStruct((16,), I32),
-            jax.ShapeDtypeStruct((COLUMNS + 1, LEAVES), I32), jax.ShapeDtypeStruct(own.shape, BF16),
+            jax.ShapeDtypeStruct((COLUMNS + 1, LEAVES), I32), jax.ShapeDtypeStruct((PAYLOAD, LANES), BF16),
         ],
-        in_specs=[HBM] * 5,
+        in_specs=[VM] * 2,
         out_specs=[VM, VM, VM, SM, VM, VM],
-        scratch_shapes=[
-            pltpu.VMEM((3, LEAVES, LANES), BF16), pltpu.VMEM((1, LEAVES), I32), pltpu.VMEM((OPS, LEAVES), I32),
-            pltpu.VMEM((COLUMNS, LEAVES), I32), pltpu.SemaphoreType.DMA((5,)),
-        ],
         compiler_params=params(24),
         name="prep",
-    )(planes, count_row, far_slots, pair_slots, own)
-
-
-def near_kernel(order, slot, lhs_ref, *refs):
+    )(own, ints)
+
+
+def near_kernel(odd_ref, order, slot, lhs_ref, *refs):
     got = refs[:PEERS]
     out_ref, w_ref, q_ref = refs[PEERS:]
     one = jnp.ones((16, LANES), BF16)
     zero = jnp.zeros((16, LANES), BF16)
     layout = spread(False, -2.0, [(0, 1.0), (1, 1.0), (2, 1.0), (3, 1.0), (4, 1.0), (5, 1.0), (6, 1.0), (6, 1.0), (6, 1.0)])
     for k in range(PEERS):
-        x, y, z, q = [got[k][c * CAP:(c + 1) * CAP, :] for c in range(4)]
+        x, y, z, q = [arrived(odd_ref[0], got, k, slice(c * CAP, (c + 1) * CAP)) for c in range(4)]
         hi, mid, lo = squares(x, y, z, 0.09)
         q_ref[k * CAP:(k + 1) * CAP, :] = q.astype(F32)
         for g in range(CAP // 16):
@@ -179,9 +206,11 @@
     w_ref[SLOTS] = one
     q_ref[SLOTS:SLOTS + 8, :] = jnp.zeros((8, LANES), F32)
     lane_row = iota((1, LANES), 1)
-    group = 16
-
-    def pair(p, rows):
+    group = 32
+
+    def pair(g, p, rows):
+        lhs = lhs_ref[group // 8 * g + p // 4][:rows, p % 4 * 32:p % 4 * 32 + 32]
+        p = g * (group // 2) + p
         tiles, charge, leaf = [], [], []
         for a in range(2):
             leaf.append(order[0, 2 * p + a])
@@ -190,7 +219,6 @@
                 t = w_ref[s]
                 tiles.append(jnp.concatenate([t, zero] if a == 0 else [zero, t], axis=0))
                 charge.append(q_ref[pl.ds(s, 1), :])
-        lhs = lhs_ref[p][:rows]
         acc = [None, None]
         for i in range(0, 2 * COLUMNS, 2):
             inv = lax.rsqrt(dot(lhs, jnp.concatenate(tiles[i:i + 2], axis=1)))
@@ -199,10 +227,9 @@
                 term = inv[:, (j - i) * LANES:(j - i + 1) * LANES] * charge[j]
                 acc[a] = term if acc[a] is None else acc[a] + term
         for a in range(2):
-            full = acc[a]
+            row = jnp.sum(acc[a].T, axis=0, keepdims=True)
             if rows < LANES:
-                full = jnp.concatenate([full, jnp.zeros((LANES - rows, LANES), F32)], axis=0)
-            row = jnp.sum(full.T, axis=0, keepdims=True)
+                row = jnp.concatenate([row, jnp.zeros((1, LANES - rows), F32)], axis=1)
             out_ref[pl.ds(leaf[a], 1), :] = jnp.where(lane_row < slot[COLUMNS, leaf[a]], row, 0.0)
 
     def body(g, _):
@@ -211,7 +238,7 @@
             @pl.when((most > rows - STEP) & (most <= rows))
             def _():
                 for p in range(group // 2):
-                    pair(g * (group // 2) + p, rows)
+                    pair(g, p, rows)
         return 0
 
     lax.fori_loop(0, LEAVES // group, body, 0)
@@ -220,31 +247,32 @@
 STEP = 32
 
 
-def near(order, pair, lhs, got):
+def near(odd, order, pair, lhs, got):
     return pl.pallas_call(
         near_kernel,
         out_shape=jax.ShapeDtypeStruct((LEAVES, LANES), F32),
-        in_specs=[SM] * 2 + [VM] * (1 + PEERS),
+        in_specs=[SM] * 3 + [VM] * (1 + PEERS),
         out_specs=VM,
         scratch_shapes=[
             pltpu.VMEM((SLOTS + 1, 16, LANES), BF16), pltpu.VMEM((SLOTS + 8, LANES), F32),
         ],
         compiler_params=params(24),
         name="near",
-    )(order, pair, lhs, *got)
-
-
-def far_kernel(tile_ref, base_ref, code_ref, m2l_h, near_ref, *refs):
+    )(odd, order, pair, lhs, *got)
+
+
+def far_kernel(tile_ref, odd_ref, base_ref, code_ref, m2l_h, near_ref, *refs):
     got = refs[:PEERS]
     part_refs = refs[PEERS:PEERS + 4]
     local, table, whole, m2l, sems = refs[PEERS + 4:]
     copies = fetch([(m2l_h, m2l)], sems)
     table[...] = jnp.zeros_like(table)
     for k in range(PEERS):
+        multi = arrived(odd_ref[0], got, k, slice(4 * CAP, 4 * CAP + CAPM))
         for b in range(CAPM // 16):
             at = base_ref[k] + 16 * b
             row = pl.multiple_of(((at >> 9) << 8) + (at & 255), 16)
-            table[(at >> 8) & 1, pl.ds(row, 16), :] = got[k][4 * CAP + 16 * b:4 * CAP + 16 * b + 16, :]
+            table[(at >> 8) & 1, pl.ds(row, 16), :] = multi[16 * b:16 * b + 16]
     local[...] = jnp.zeros_like(local)
     whole[:, :LANES] = table[0]
     whole[:, LANES:] = table[1]
@@ -291,11 +319,11 @@
         part_refs[d][:, LANES:] = local[pl.ds(at, rows), :]
 
 
-def far(tile, base, code, m2l, near_part, got):
+def far(tile, odd, base, code, m2l, near_part, got):
     return pl.pallas_call(
         far_kernel,
         out_shape=[jax.ShapeDtypeStruct((LEAVES // 4, 2 * LANES), F32)] * 4,
-        in_specs=[SM, SM, VM, HBM, VM] + [VM] * PEERS,
+        in_specs=[SM, SM, SM, VM, HBM, VM] + [VM] * PEERS,
         out_specs=[VM] * 4,
         scratch_shapes=[
             pltpu.VMEM((LEAVES, LANES), F32), pltpu.VMEM((2, TABLE, LANES), BF16),
@@ -304,7 +332,7 @@
         ],
         compiler_params=params(32),
         name="far",
-    )(tile, base, code, m2l, near_part, *got)
+    )(tile, odd, base, code, m2l, near_part, *got)
 
 
 def per_device(positions, charges, leaf_counts, multipoles, m2l_ops, leaf_send, pair_slots, far_send, far_slots):
@@ -313,16 +341,19 @@
     tiles = lax.axis_size("tile")
     planes = jnp.transpose(positions, (1, 0, 2))
     count_row = leaf_counts.reshape(1, LEAVES)
-    payload = pack(planes, charges, count_row, multipoles, leaf_send, far_send)
+    odd = lax.rem(lax.axis_index("slab").astype(I32), 2).reshape(1)
+    *payload, ints = pack(
+        odd, planes, charges, count_row, multipoles, leaf_send, far_send, far_slots.T, pair_slots.T)
     got = list(payload)
-    for step in range(reach, 0, -1):
-        for k in (reach + step, reach - step):
-            hops = k - reach
-            got[k] = lax.ppermute(payload[k], "slab", [(s, (s + hops) % slabs) for s in range(slabs)])
-    lhs, order, code, base, pair, got[reach] = prep(planes, count_row, far_slots.T, pair_slots.T, payload[reach])
-    near_part = near(order, pair, lhs, got)
+    for i, (low, high) in enumerate(routes()):
+        hops = high - reach
+        if hops:
+            pairs = [(s, (s + (hops if s % 2 == 0 else -hops)) % slabs) for s in range(slabs)]
+            got[i] = lax.ppermute(payload[i], "slab", pairs)
+    lhs, order, code, base, pair, got[0] = prep(payload[0], ints)
+    near_part = near(odd, order, pair, lhs, got)
     tile = lax.axis_index("tile").astype(I32).reshape(1)
-    parts = far(tile, base, code, m2l_ops, near_part, got)
+    parts = far(tile, odd, base, code, m2l_ops, near_part, got)
     total = parts[0]
     for step in range(1, tiles):
         total = total + lax.ppermute(parts[step], "tile", [(t, (t + step) % tiles) for t in range(tiles)])

time: 75.8 us -> 68.5 us (0.904); the launches traced: 74.7 us -> 68.3 us
  starting transfers between devices: 14.2 us -> 24 us
  waiting for transfers between devices: 17.6 us -> 8.11 us
  Pallas kernels: 37.4 us -> 33 us
  local copies, waits for them, and re-layouts: 4.72 us -> 2.49 us
    ppermute x8, starting transfers between devices: 10.7 us -> 21 us  [per_device(): got[i] = lax.ppermute(payload[i], 'slab', pairs)]
    ppermute x8, waiting for transfers between devices: 12 us -> 2.64 us  [per_device(): got[i] = lax.ppermute(payload[i], 'slab', pairs)]
    unnamed x12 -> x6, local copies, waits for them, and re-layouts: 4.09 us -> 1.86 us
    pallas_call x2, Pallas kernels: 6.77 us -> 4.82 us  [the longest x1 3.04 us: pack(): pl.pallas_call(pack_kernel, out_shape=[jax.ShapeDtypeStruct((PAYLOAD + 3...]
    pallas_call x1, Pallas kernels: 17.6 us -> 16.1 us  [near(): pl.pallas_call(near_kernel, out_shape=jax.ShapeDtypeStruct((LEAVES, LANES...]
    pallas_call x1, Pallas kernels: 13.1 us -> 12 us  [far(): pl.pallas_call(far_kernel, out_shape=[jax.ShapeDtypeStruct((LEAVES // 4,...]
  transfers between devices with their start and end apart: 11 -> 11, of which waited for: 7 -> 4; matrix products, arithmetic and copies ran while one was open for 0% -> 0% of each run, Pallas kernels for 5% -> 3%
where the time goes in v3:
time: 68.5 us; the launch traced here: 68.3 us
  Pallas kernels  33 us (48%)
  starting transfers between devices  24 us (35%)
  waiting for transfers between devices  8.11 us (12%)
  local copies, waits for them, and re-layouts  2.49 us (4%)
  between operations  0.73 us (1%)
    ppermute x8, starting transfers between devices, per_device(): got[i] = lax.ppermute(payload[i], 'slab', pairs)  21 us
    pallas_call x1, Pallas kernels, near(): pl.pallas_call(near_kernel, out_shape=jax.ShapeDtypeStruct((LEAVES, LANES...  16.1 us
    pallas_call x1, Pallas kernels, far(): pl.pallas_call(far_kernel, out_shape=[jax.ShapeDtypeStruct((LEAVES // 4,...  12 us
    ppermute x3, waiting for transfers between devices, per_device(): lax.ppermute(parts[step], 'tile', [(t, (t + step) % tiles) for t in range...  5.47 us
    pallas_call x1, Pallas kernels, pack(): pl.pallas_call(pack_kernel, out_shape=[jax.ShapeDtypeStruct((PAYLOAD + 3...  3.04 us
    ppermute x3, starting transfers between devices, per_device(): lax.ppermute(parts[step], 'tile', [(t, (t + step) % tiles) for t in range...  2.98 us
    ppermute x8, waiting for transfers between devices, per_device(): got[i] = lax.ppermute(payload[i], 'slab', pairs)  2.64 us
    unnamed x6, local copies, waits for them, and re-layouts  1.86 us
  transfers between devices with their start and end apart: 11, of which 4 were waited for; matrix products, arithmetic and copies ran while one was open for 0% of the time, Pallas kernels for 3%

profile of v3, /device:TPU:6, one launch (start us, length us, event | category | flops | bytes accessed | tf_op | source)
XLA Modules:
  0.0 68.3 jit_solution(17150325630435532662)
XLA Ops:
  0.6 0.0 copy-start
  0.6 3.0 %pack.1 = (bf16[1216,128]{1,0:T(8,128)(2,1)}, bf16[448,128]{1,0:T(8,128)(2,1)}, bf16[448,128]{1,0:T(8,128)(2,1)}, bf16[448,128]{1,0:T(8,128)(2,1)}, bf16[448,128...) custom-call(s32[1]{0:T(128)} %bitcast.1.odd_ref, ...), custom_call_target="tpu_custom_call" | custom-call | tf_op jit(solution)/shard_map/pack/pallas_call | solution.py:97
  3.7 3.3 %collective-permute-start = (bf16[448,128]{1,0:T(8,128)(2,1)}, bf16[448,128]{1,0:T(8,128)(2,1)S(1)}, u32[]{:S(2)}, u32[]{:S(2)}) collective-permute-start(bf16[448,128]{1,0:T(8,128)(2,1)} %get-tuple-element.30), channel_id=1, source_target_pairs={{0,16},{4,244},{8,24},{12,252},{16,32},{20,4},{24,40},{28,12},{32,... | collective-permute-start | bytes 344072 | tf_op jit(solution)/shard_map/ppermute | solution.py:352
  7.1 5.6 %collective-permute-start.1 = (bf16[448,128]{1,0:T(8,128)(2,1)}, bf16[448,128]{1,0:T(8,128)(2,1)S(1)}, u32[]{:S(2)}, u32[]{:S(2)}) collective-permute-start(bf16[448,128]{1,0:T(8,128)(2,1)} %get-tuple-element.31), channel_id=1, source_target_pairs={{0,240},{4,20},{8,248},{12,28},{16,0},{20,36},{24,8},{28,44},{32,1... | collective-permute-start | bytes 344072 | tf_op jit(solution)/shard_map/ppermute | solution.py:352
  12.6 0.1 collective-permute-start.2
  12.7 4.9 %collective-permute-start.3 = (bf16[448,128]{1,0:T(8,128)(2,1)}, bf16[448,128]{1,0:T(8,128)(2,1)S(1)}, u32[]{:S(2)}, u32[]{:S(2)}) collective-permute-start(bf16[448,128]{1,0:T(8,128)(2,1)} %get-tuple-element.33), channel_id=1, source_target_pairs={{0,244},{4,16},{8,252},{12,24},{16,4},{20,32},{24,12},{28,40},{32,... | collective-permute-start | bytes 344072 | tf_op jit(solution)/shard_map/ppermute | solution.py:352
  17.7 1.0 %collective-permute-start.4 = (bf16[448,128]{1,0:T(8,128)(2,1)}, bf16[448,128]{1,0:T(8,128)(2,1)S(1)}, u32[]{:S(2)}, u32[]{:S(2)}) collective-permute-start(bf16[448,128]{1,0:T(8,128)(2,1)} %get-tuple-element.34), channel_id=1, source_target_pairs={{0,8},{4,252},{8,16},{12,4},{16,24},{20,12},{24,32},{28,20},{32,40... | collective-permute-start | bytes 344072 | tf_op jit(solution)/shard_map/ppermute | solution.py:352
  18.7 0.0 collective-permute-done.refs_1_
  18.7 4.3 %collective-permute-start.5 = (bf16[448,128]{1,0:T(8,128)(2,1)}, bf16[448,128]{1,0:T(8,128)(2,1)S(1)}, u32[]{:S(2)}, u32[]{:S(2)}) collective-permute-start(bf16[448,128]{1,0:T(8,128)(2,1)} %get-tuple-element.35), channel_id=1, source_target_pairs={{0,248},{4,12},{8,0},{12,20},{16,8},{20,28},{24,16},{28,36},{32,24... | collective-permute-start | bytes 344072 | tf_op jit(solution)/shard_map/ppermute | solution.py:352
  23.0 0.0 collective-permute-done.1.refs_2_
  23.0 0.0 collective-permute-start.6
  23.0 0.0 collective-permute-done.2.refs_3_
  23.0 1.7 %collective-permute-start.7 = (bf16[448,128]{1,0:T(8,128)(2,1)}, bf16[448,128]{1,0:T(8,128)(2,1)S(1)}, u32[]{:S(2)}, u32[]{:S(2)}) collective-permute-start(bf16[448,128]{1,0:T(8,128)(2,1)} %get-tuple-element.37), channel_id=1, source_target_pairs={{0,252},{4,8},{8,4},{12,16},{16,12},{20,24},{24,20},{28,32},{32,28... | collective-permute-start | bytes 344072 | tf_op jit(solution)/shard_map/ppermute | solution.py:352
  24.7 0.0 copy-start.1
  24.7 1.0 %copy-done.1 = bf16[1216,128]{1,0:T(8,128)(2,1)S(1)} copy-done((bf16[1216,128]{1,0:T(8,128)(2,1)S(1)}, bf16[1216,128]{1,0:T(8,128)(2,1)}, u32[]{:S(2)}) %copy-start.1) | copy-done | bytes 311320
  25.7 0.0 copy-start.2
  25.7 0.9 %copy-done.2 = s32[96,256]{1,0:T(8,128)S(1)} copy-done((s32[96,256]{1,0:T(8,128)S(1)}, s32[96,256]{1,0:T(8,128)}, u32[]{:S(2)}) %copy-start.2) | copy-done | bytes 98328
  26.6 1.8 %prep.1 = (bf16[32,128,128]{2,1,0:T(8,128)(2,1)S(1)}, s32[8,256]{1,0:T(8,128)S(1)}, f32[256,128]{1,0:T(8,128)S(1)}, s32[16]{0:T(128)S(1)}, s32[8,256]{1,0:T(8,128)S(1)}, /*index=5*/bf16[448,128]{1,0:T(8,128)(2,1)S(1)}) custom-call(bf16[1216,128]{1,0:T(8,128)(2,1)S(1)} %copy-done.1, s32[96,256]{1,0:T(8,128)S(1)} %copy-done.2), custom_call_target="tpu_custom_call" | custom-call | tf_op jit(solution)/shard_map/prep/pallas_call | solution.py:178
  28.4 0.0 collective-permute-done.3.refs_4_
  28.4 0.0 collective-permute-done.4.refs_5_
  28.4 0.0 collective-permute-done.5.refs_6_
  28.4 0.0 collective-permute-done.6.refs_7_
  28.4 2.6 %collective-permute-done.7.refs_8_ = bf16[448,128]{1,0:T(8,128)(2,1)S(1)} collective-permute-done((bf16[448,128]{1,0:T(8,128)(2,1)}, bf16[448,128]{1,0:T(8,128)(2,1)S(1)}, u32[]{:S(2)}, u32[]{:S(2)}) %collective-permute-start.7) | collective-permute-done | bytes 114720 | tf_op jit(solution)/shard_map/ppermute | solution.py:352
  31.0 16.1 %near.1.near_ref = f32[256,128]{1,0:T(8,128)S(1)} custom-call(s32[1]{0:T(128)} %bitcast.1.odd_ref, s32[8,256]{1,0:T(8,128)S(1)} %get-tuple-element.26.order, s32[8,256]{1,0:T(8,128)S(1)} %get-tuple-element.27.slot, bf16[32,128,128]{2,1,0:T(8,128)(2,1)S(1)} %get-tuple-element.28.lhs_ref, bf16[448,128]{1,0:T(8,128)(2,1)S(1)} %get-tuple-element.29.refs_0_, ...), custom_call_target="tpu_custom_call" | custom-call | tf_op jit(solution)/shard_map/near/pallas_call | solution.py:251
  47.2 0.0 copy-done
  47.2 12.0 %far.1 = (f32[64,256]{1,0:T(8,128)S(1)}, f32[64,256]{1,0:T(8,128)S(1)}, f32[64,256]{1,0:T(8,128)S(1)}, f32[64,256]{1,0:T(8,128)S(1)}) custom-call(s32[1]{0:T(128)} %bitcast.tile_ref, s32[1]{0:T(128)} %bitcast.1.odd_ref, s32[16]{0:T(128)S(1)} %get-tuple-element.24.base_ref, f32[256,128]{1,0:T(8,128)S(1)} %get-tuple-element.25.code_ref, ...), custom_call_target="tpu_custom_call" | custom-call | tf_op jit(solution)/shard_map/far/pallas_call | solution.py:323
  59.2 0.6 collective-permute-start.8
  59.8 2.4 %collective-permute-start.9 = (f32[64,256]{1,0:T(8,128)S(1)}, f32[64,256]{1,0:T(8,128)S(1)}, u32[]{:S(2)}, u32[]{:S(2)}) collective-permute-start(f32[64,256]{1,0:T(8,128)S(1)} %get-tuple-element.40), channel_id=1, source_target_pairs={{0,2},{1,3},{2,0},{3,1},{4,6},{5,7},{6,4},{7,5},{8,10},{9,11},{10,... | collective-permute-start | bytes 196616 | tf_op jit(solution)/shard_map/ppermute | solution.py:359
  62.2 0.0 collective-permute-start.10
  62.2 1.4 %collective-permute-done.8 = f32[64,256]{1,0:T(8,128)S(1)} collective-permute-done((f32[64,256]{1,0:T(8,128)S(1)}, f32[64,256]{1,0:T(8,128)S(1)}, u32[]{:S(2)}, u32[]{:S(2)}) %collective-permute-start.8) | collective-permute-done | bytes 65568 | tf_op jit(solution)/shard_map/ppermute | solution.py:359
  63.5 2.0 %collective-permute-done.9 = f32[64,256]{1,0:T(8,128)S(1)} collective-permute-done((f32[64,256]{1,0:T(8,128)S(1)}, f32[64,256]{1,0:T(8,128)S(1)}, u32[]{:S(2)}, u32[]{:S(2)}) %collective-permute-start.9) | collective-permute-done | bytes 65568 | tf_op jit(solution)/shard_map/ppermute | solution.py:359
  65.5 2.1 %collective-permute-done.10 = f32[64,256]{1,0:T(8,128)S(1)} collective-permute-done((f32[64,256]{1,0:T(8,128)S(1)}, f32[64,256]{1,0:T(8,128)S(1)}, u32[]{:S(2)}, u32[]{:S(2)}) %collective-permute-start.10) | collective-permute-done | bytes 65568 | tf_op jit(solution)/shard_map/ppermute | solution.py:359
  67.7 0.6 fusion
  (1 shorter events, 0.0 us)
Async XLA Ops:
  0.6 46.5 %copy-start = (bf16[79,128,128]{2,1,0:T(8,128)(2,1)S(1)}, bf16[79,128,128]{2,1,0:T(8,128)(2,1)}, u32[]{:S(2)}) copy-start(bf16[79,128,128]{2,1,0:T(8,128)(2,1)} %m2l_h.1) | copy-start | bytes 7766020
  3.7 15.0 %collective-permute-start = (bf16[448,128]{1,0:T(8,128)(2,1)}, bf16[448,128]{1,0:T(8,128)(2,1)S(1)}, u32[]{:S(2)}, u32[]{:S(2)}) collective-permute-start(bf16[448,128]{1,0:T(8,128)(2,1)} %get-tuple-element.30), channel_id=1, source_target_pairs={{0,16},{4,244},{8,24},{12,252},{16,32},{20,4},{24,40},{28,12},{32,... | collective-permute-start | bytes 344072 | tf_op jit(solution)/shard_map/ppermute | solution.py:352
  7.1 16.0 %collective-permute-start.1 = (bf16[448,128]{1,0:T(8,128)(2,1)}, bf16[448,128]{1,0:T(8,128)(2,1)S(1)}, u32[]{:S(2)}, u32[]{:S(2)}) collective-permute-start(bf16[448,128]{1,0:T(8,128)(2,1)} %get-tuple-element.31), channel_id=1, source_target_pairs={{0,240},{4,20},{8,248},{12,28},{16,0},{20,36},{24,8},{28,44},{32,1... | collective-permute-start | bytes 344072 | tf_op jit(solution)/shard_map/ppermute | solution.py:352
  12.6 10.4 %collective-permute-start.2 = (bf16[448,128]{1,0:T(8,128)(2,1)}, bf16[448,128]{1,0:T(8,128)(2,1)S(1)}, u32[]{:S(2)}, u32[]{:S(2)}) collective-permute-start(bf16[448,128]{1,0:T(8,128)(2,1)} %get-tuple-element.32), channel_id=1, source_target_pairs={{0,12},{4,248},{8,20},{12,0},{16,28},{20,8},{24,36},{28,16},{32,44... | collective-permute-start | bytes 344072 | tf_op jit(solution)/shard_map/ppermute | solution.py:352
  12.7 15.7 %collective-permute-start.3 = (bf16[448,128]{1,0:T(8,128)(2,1)}, bf16[448,128]{1,0:T(8,128)(2,1)S(1)}, u32[]{:S(2)}, u32[]{:S(2)}) collective-permute-start(bf16[448,128]{1,0:T(8,128)(2,1)} %get-tuple-element.33), channel_id=1, source_target_pairs={{0,244},{4,16},{8,252},{12,24},{16,4},{20,32},{24,12},{28,40},{32,... | collective-permute-start | bytes 344072 | tf_op jit(solution)/shard_map/ppermute | solution.py:352
  17.7 10.7 %collective-permute-start.4 = (bf16[448,128]{1,0:T(8,128)(2,1)}, bf16[448,128]{1,0:T(8,128)(2,1)S(1)}, u32[]{:S(2)}, u32[]{:S(2)}) collective-permute-start(bf16[448,128]{1,0:T(8,128)(2,1)} %get-tuple-element.34), channel_id=1, source_target_pairs={{0,8},{4,252},{8,16},{12,4},{16,24},{20,12},{24,32},{28,20},{32,40... | collective-permute-start | bytes 344072 | tf_op jit(solution)/shard_map/ppermute | solution.py:352
  18.7 9.7 %collective-permute-start.5 = (bf16[448,128]{1,0:T(8,128)(2,1)}, bf16[448,128]{1,0:T(8,128)(2,1)S(1)}, u32[]{:S(2)}, u32[]{:S(2)}) collective-permute-start(bf16[448,128]{1,0:T(8,128)(2,1)} %get-tuple-element.35), channel_id=1, source_target_pairs={{0,248},{4,12},{8,0},{12,20},{16,8},{20,28},{24,16},{28,36},{32,24... | collective-permute-start | bytes 344072 | tf_op jit(solution)/shard_map/ppermute | solution.py:352
  23.0 5.4 %collective-permute-start.6 = (bf16[448,128]{1,0:T(8,128)(2,1)}, bf16[448,128]{1,0:T(8,128)(2,1)S(1)}, u32[]{:S(2)}, u32[]{:S(2)}) collective-permute-start(bf16[448,128]{1,0:T(8,128)(2,1)} %get-tuple-element.36), channel_id=1, source_target_pairs={{0,4},{4,0},{8,12},{12,8},{16,20},{20,16},{24,28},{28,24},{32,36},... | collective-permute-start | bytes 344072 | tf_op jit(solution)/shard_map/ppermute | solution.py:352
  23.0 8.0 %collective-permute-start.7 = (bf16[448,128]{1,0:T(8,128)(2,1)}, bf16[448,128]{1,0:T(8,128)(2,1)S(1)}, u32[]{:S(2)}, u32[]{:S(2)}) collective-permute-start(bf16[448,128]{1,0:T(8,128)(2,1)} %get-tuple-element.37), channel_id=1, source_target_pairs={{0,252},{4,8},{8,4},{12,16},{16,12},{20,24},{24,20},{28,32},{32,28... | collective-permute-start | bytes 344072 | tf_op jit(solution)/shard_map/ppermute | solution.py:352
  24.7 1.0 %copy-start.1 = (bf16[1216,128]{1,0:T(8,128)(2,1)S(1)}, bf16[1216,128]{1,0:T(8,128)(2,1)}, u32[]{:S(2)}) copy-start(bf16[1216,128]{1,0:T(8,128)(2,1)} %get-tuple-element.22.own_in_ref) | copy-start | bytes 933892
  25.7 0.9 %copy-start.2 = (s32[96,256]{1,0:T(8,128)S(1)}, s32[96,256]{1,0:T(8,128)}, u32[]{:S(2)}) copy-start(s32[96,256]{1,0:T(8,128)} %get-tuple-element.23.ints_ref) | copy-start | bytes 294916
  59.2 4.3 %collective-permute-start.8 = (f32[64,256]{1,0:T(8,128)S(1)}, f32[64,256]{1,0:T(8,128)S(1)}, u32[]{:S(2)}, u32[]{:S(2)}) collective-permute-start(f32[64,256]{1,0:T(8,128)S(1)} %get-tuple-element.39), channel_id=1, source_target_pairs={{0,1},{1,2},{2,3},{3,0},{4,5},{5,6},{6,7},{7,4},{8,9},{9,10},{10,1... | collective-permute-start | bytes 196616 | tf_op jit(solution)/shard_map/ppermute | solution.py:359
  59.8 5.8 %collective-permute-start.9 = (f32[64,256]{1,0:T(8,128)S(1)}, f32[64,256]{1,0:T(8,128)S(1)}, u32[]{:S(2)}, u32[]{:S(2)}) collective-permute-start(f32[64,256]{1,0:T(8,128)S(1)} %get-tuple-element.40), channel_id=1, source_target_pairs={{0,2},{1,3},{2,0},{3,1},{4,6},{5,7},{6,4},{7,5},{8,10},{9,11},{10,... | collective-permute-start | bytes 196616 | tf_op jit(solution)/shard_map/ppermute | solution.py:359
  62.2 5.5 %collective-permute-start.10 = (f32[64,256]{1,0:T(8,128)S(1)}, f32[64,256]{1,0:T(8,128)S(1)}, u32[]{:S(2)}, u32[]{:S(2)}) collective-permute-start(f32[64,256]{1,0:T(8,128)S(1)} %get-tuple-element.41), channel_id=1, source_target_pairs={{0,3},{1,0},{2,1},{3,2},{4,7},{5,4},{6,5},{7,6},{8,11},{9,8},{10,9... | collective-permute-start | bytes 196616 | tf_op jit(solution)/shard_map/ppermute | solution.py:359

commit v4 on v3

--- a/solution.py
+++ b/solution.py
@@ -314,7 +314,7 @@
 
     rows = LEAVES // 4
     for d in range(4):
-        at = pl.multiple_of(lax.rem(tile_ref[0] + d, 4) * rows, rows)
+        at = pl.multiple_of(lax.rem(tile_ref[0] + jnp.where(odd_ref[0] == 0, d, 4 - d), 4) * rows, rows)
         part_refs[d][:, :LANES] = near_ref[pl.ds(at, rows), :]
         part_refs[d][:, LANES:] = local[pl.ds(at, rows), :]
 
@@ -356,7 +356,11 @@
     parts = far(tile, odd, base, code, m2l_ops, near_part, got)
     total = parts[0]
     for step in range(1, tiles):
-        total = total + lax.ppermute(parts[step], "tile", [(t, (t + step) % tiles) for t in range(tiles)])
+        pairs = [
+            (r * tiles + t, r * tiles + (t + (step if r % 2 == 0 else -step)) % tiles)
+            for r in range(slabs) for t in range(tiles)
+        ]
+        total = total + lax.ppermute(parts[step], ("slab", "tile"), pairs)
     return total[:, :LANES], total[:, LANES:]
 
 

time: 68.5 us -> 68 us (level)
  no operation moved by 1% of the time
where the time goes in v4:
time: 68 us; the launch traced here: 68.3 us
  Pallas kernels  33 us (49%)
  starting transfers between devices  24 us (35%)
  waiting for transfers between devices  8.11 us (12%)
  local copies, waits for them, and re-layouts  2.49 us (4%)
  between operations  0.73 us (1%)
    ppermute x8, starting transfers between devices, per_device(): got[i] = lax.ppermute(payload[i], 'slab', pairs)  21 us
    pallas_call x1, Pallas kernels, near(): pl.pallas_call(near_kernel, out_shape=jax.ShapeDtypeStruct((LEAVES, LANES...  16.1 us
    pallas_call x1, Pallas kernels, far(): pl.pallas_call(far_kernel, out_shape=[jax.ShapeDtypeStruct((LEAVES // 4,...  12 us
    ppermute x3, waiting for transfers between devices, per_device(): total = total + lax.ppermute(parts[step], ('slab', 'tile'), pairs)  5.47 us
    pallas_call x1, Pallas kernels, pack(): pl.pallas_call(pack_kernel, out_shape=[jax.ShapeDtypeStruct((PAYLOAD + 3...  3.04 us
    ppermute x3, starting transfers between devices, per_device(): total = total + lax.ppermute(parts[step], ('slab', 'tile'), pairs)  3.01 us
    ppermute x8, waiting for transfers between devices, per_device(): got[i] = lax.ppermute(payload[i], 'slab', pairs)  2.64 us
    unnamed x6, local copies, waits for them, and re-layouts  1.86 us
  transfers between devices with their start and end apart: 11, of which 4 were waited for; matrix products, arithmetic and copies ran while one was open for 0% of the time, Pallas kernels for 3%

profile of v4, /device:TPU:6, one launch (start us, length us, event | category | flops | bytes accessed | tf_op | source)
XLA Modules:
  0.0 68.3 jit_solution(13741862926449116367)
XLA Ops:
  0.6 0.0 copy-start
  0.6 3.0 %pack.1 = (bf16[1216,128]{1,0:T(8,128)(2,1)}, bf16[448,128]{1,0:T(8,128)(2,1)}, bf16[448,128]{1,0:T(8,128)(2,1)}, bf16[448,128]{1,0:T(8,128)(2,1)}, bf16[448,128...) custom-call(s32[1]{0:T(128)} %bitcast.1.odd_ref, ...), custom_call_target="tpu_custom_call" | custom-call | tf_op jit(solution)/shard_map/pack/pallas_call | solution.py:97
  3.7 3.3 %collective-permute-start = (bf16[448,128]{1,0:T(8,128)(2,1)}, bf16[448,128]{1,0:T(8,128)(2,1)S(1)}, u32[]{:S(2)}, u32[]{:S(2)}) collective-permute-start(bf16[448,128]{1,0:T(8,128)(2,1)} %get-tuple-element.30), channel_id=1, source_target_pairs={{0,16},{4,244},{8,24},{12,252},{16,32},{20,4},{24,40},{28,12},{32,... | collective-permute-start | bytes 344072 | tf_op jit(solution)/shard_map/ppermute | solution.py:352
  7.1 5.6 %collective-permute-start.1 = (bf16[448,128]{1,0:T(8,128)(2,1)}, bf16[448,128]{1,0:T(8,128)(2,1)S(1)}, u32[]{:S(2)}, u32[]{:S(2)}) collective-permute-start(bf16[448,128]{1,0:T(8,128)(2,1)} %get-tuple-element.31), channel_id=1, source_target_pairs={{0,240},{4,20},{8,248},{12,28},{16,0},{20,36},{24,8},{28,44},{32,1... | collective-permute-start | bytes 344072 | tf_op jit(solution)/shard_map/ppermute | solution.py:352
  12.6 0.1 collective-permute-start.2
  12.7 4.9 %collective-permute-start.3 = (bf16[448,128]{1,0:T(8,128)(2,1)}, bf16[448,128]{1,0:T(8,128)(2,1)S(1)}, u32[]{:S(2)}, u32[]{:S(2)}) collective-permute-start(bf16[448,128]{1,0:T(8,128)(2,1)} %get-tuple-element.33), channel_id=1, source_target_pairs={{0,244},{4,16},{8,252},{12,24},{16,4},{20,32},{24,12},{28,40},{32,... | collective-permute-start | bytes 344072 | tf_op jit(solution)/shard_map/ppermute | solution.py:352
  17.7 1.0 %collective-permute-start.4 = (bf16[448,128]{1,0:T(8,128)(2,1)}, bf16[448,128]{1,0:T(8,128)(2,1)S(1)}, u32[]{:S(2)}, u32[]{:S(2)}) collective-permute-start(bf16[448,128]{1,0:T(8,128)(2,1)} %get-tuple-element.34), channel_id=1, source_target_pairs={{0,8},{4,252},{8,16},{12,4},{16,24},{20,12},{24,32},{28,20},{32,40... | collective-permute-start | bytes 344072 | tf_op jit(solution)/shard_map/ppermute | solution.py:352
  18.7 0.0 collective-permute-done.refs_1_
  18.7 4.3 %collective-permute-start.5 = (bf16[448,128]{1,0:T(8,128)(2,1)}, bf16[448,128]{1,0:T(8,128)(2,1)S(1)}, u32[]{:S(2)}, u32[]{:S(2)}) collective-permute-start(bf16[448,128]{1,0:T(8,128)(2,1)} %get-tuple-element.35), channel_id=1, source_target_pairs={{0,248},{4,12},{8,0},{12,20},{16,8},{20,28},{24,16},{28,36},{32,24... | collective-permute-start | bytes 344072 | tf_op jit(solution)/shard_map/ppermute | solution.py:352
  23.0 0.0 collective-permute-done.1.refs_2_
  23.0 0.0 collective-permute-start.6
  23.0 0.0 collective-permute-done.2.refs_3_
  23.0 1.7 %collective-permute-start.7 = (bf16[448,128]{1,0:T(8,128)(2,1)}, bf16[448,128]{1,0:T(8,128)(2,1)S(1)}, u32[]{:S(2)}, u32[]{:S(2)}) collective-permute-start(bf16[448,128]{1,0:T(8,128)(2,1)} %get-tuple-element.37), channel_id=1, source_target_pairs={{0,252},{4,8},{8,4},{12,16},{16,12},{20,24},{24,20},{28,32},{32,28... | collective-permute-start | bytes 344072 | tf_op jit(solution)/shard_map/ppermute | solution.py:352
  24.7 0.0 copy-start.1
  24.7 1.0 %copy-done.1 = bf16[1216,128]{1,0:T(8,128)(2,1)S(1)} copy-done((bf16[1216,128]{1,0:T(8,128)(2,1)S(1)}, bf16[1216,128]{1,0:T(8,128)(2,1)}, u32[]{:S(2)}) %copy-start.1) | copy-done | bytes 311320
  25.7 0.0 copy-start.2
  25.7 0.9 %copy-done.2 = s32[96,256]{1,0:T(8,128)S(1)} copy-done((s32[96,256]{1,0:T(8,128)S(1)}, s32[96,256]{1,0:T(8,128)}, u32[]{:S(2)}) %copy-start.2) | copy-done | bytes 98328
  26.6 1.8 %prep.1 = (bf16[32,128,128]{2,1,0:T(8,128)(2,1)S(1)}, s32[8,256]{1,0:T(8,128)S(1)}, f32[256,128]{1,0:T(8,128)S(1)}, s32[16]{0:T(128)S(1)}, s32[8,256]{1,0:T(8,128)S(1)}, /*index=5*/bf16[448,128]{1,0:T(8,128)(2,1)S(1)}) custom-call(bf16[1216,128]{1,0:T(8,128)(2,1)S(1)} %copy-done.1, s32[96,256]{1,0:T(8,128)S(1)} %copy-done.2), custom_call_target="tpu_custom_call" | custom-call | tf_op jit(solution)/shard_map/prep/pallas_call | solution.py:178
  28.4 0.0 collective-permute-done.3.refs_4_
  28.4 0.0 collective-permute-done.4.refs_5_
  28.4 0.0 collective-permute-done.5.refs_6_
  28.4 0.0 collective-permute-done.6.refs_7_
  28.4 2.6 %collective-permute-done.7.refs_8_ = bf16[448,128]{1,0:T(8,128)(2,1)S(1)} collective-permute-done((bf16[448,128]{1,0:T(8,128)(2,1)}, bf16[448,128]{1,0:T(8,128)(2,1)S(1)}, u32[]{:S(2)}, u32[]{:S(2)}) %collective-permute-start.7) | collective-permute-done | bytes 114720 | tf_op jit(solution)/shard_map/ppermute | solution.py:352
  31.0 16.1 %near.1.near_ref = f32[256,128]{1,0:T(8,128)S(1)} custom-call(s32[1]{0:T(128)} %bitcast.1.odd_ref, s32[8,256]{1,0:T(8,128)S(1)} %get-tuple-element.26.order, s32[8,256]{1,0:T(8,128)S(1)} %get-tuple-element.27.slot, bf16[32,128,128]{2,1,0:T(8,128)(2,1)S(1)} %get-tuple-element.28.lhs_ref, bf16[448,128]{1,0:T(8,128)(2,1)S(1)} %get-tuple-element.29.refs_0_, ...), custom_call_target="tpu_custom_call" | custom-call | tf_op jit(solution)/shard_map/near/pallas_call | solution.py:251
  47.2 0.0 copy-done
  47.2 12.0 %far.1 = (f32[64,256]{1,0:T(8,128)S(1)}, f32[64,256]{1,0:T(8,128)S(1)}, f32[64,256]{1,0:T(8,128)S(1)}, f32[64,256]{1,0:T(8,128)S(1)}) custom-call(s32[1]{0:T(128)} %bitcast.tile_ref, s32[1]{0:T(128)} %bitcast.1.odd_ref, s32[16]{0:T(128)S(1)} %get-tuple-element.24.base_ref, f32[256,128]{1,0:T(8,128)S(1)} %get-tuple-element.25.code_ref, ...), custom_call_target="tpu_custom_call" | custom-call | tf_op jit(solution)/shard_map/far/pallas_call | solution.py:323
  59.2 0.6 collective-permute-start.8
  59.8 2.4 %collective-permute-start.9 = (f32[64,256]{1,0:T(8,128)S(1)}, f32[64,256]{1,0:T(8,128)S(1)}, u32[]{:S(2)}, u32[]{:S(2)}) collective-permute-start(f32[64,256]{1,0:T(8,128)S(1)} %get-tuple-element.40), channel_id=1, source_target_pairs={{0,2},{1,3},{2,0},{3,1},{4,6},{5,7},{6,4},{7,5},{8,10},{9,11},{10,... | collective-permute-start | bytes 196616 | tf_op jit(solution)/shard_map/ppermute | solution.py:363
  62.2 0.0 collective-permute-start.10
  62.2 1.3 %collective-permute-done.8 = f32[64,256]{1,0:T(8,128)S(1)} collective-permute-done((f32[64,256]{1,0:T(8,128)S(1)}, f32[64,256]{1,0:T(8,128)S(1)}, u32[]{:S(2)}, u32[]{:S(2)}) %collective-permute-start.8) | collective-permute-done | bytes 65568 | tf_op jit(solution)/shard_map/ppermute | solution.py:363
  63.5 2.0 %collective-permute-done.9 = f32[64,256]{1,0:T(8,128)S(1)} collective-permute-done((f32[64,256]{1,0:T(8,128)S(1)}, f32[64,256]{1,0:T(8,128)S(1)}, u32[]{:S(2)}, u32[]{:S(2)}) %collective-permute-start.9) | collective-permute-done | bytes 65568 | tf_op jit(solution)/shard_map/ppermute | solution.py:363
  65.5 2.1 %collective-permute-done.10 = f32[64,256]{1,0:T(8,128)S(1)} collective-permute-done((f32[64,256]{1,0:T(8,128)S(1)}, f32[64,256]{1,0:T(8,128)S(1)}, u32[]{:S(2)}, u32[]{:S(2)}) %collective-permute-start.10) | collective-permute-done | bytes 65568 | tf_op jit(solution)/shard_map/ppermute | solution.py:363
  67.7 0.6 fusion
  (1 shorter events, 0.0 us)
Async XLA Ops:
  0.6 46.5 %copy-start = (bf16[79,128,128]{2,1,0:T(8,128)(2,1)S(1)}, bf16[79,128,128]{2,1,0:T(8,128)(2,1)}, u32[]{:S(2)}) copy-start(bf16[79,128,128]{2,1,0:T(8,128)(2,1)} %m2l_h.1) | copy-start | bytes 7766020
  3.7 15.0 %collective-permute-start = (bf16[448,128]{1,0:T(8,128)(2,1)}, bf16[448,128]{1,0:T(8,128)(2,1)S(1)}, u32[]{:S(2)}, u32[]{:S(2)}) collective-permute-start(bf16[448,128]{1,0:T(8,128)(2,1)} %get-tuple-element.30), channel_id=1, source_target_pairs={{0,16},{4,244},{8,24},{12,252},{16,32},{20,4},{24,40},{28,12},{32,... | collective-permute-start | bytes 344072 | tf_op jit(solution)/shard_map/ppermute | solution.py:352
  7.1 16.0 %collective-permute-start.1 = (bf16[448,128]{1,0:T(8,128)(2,1)}, bf16[448,128]{1,0:T(8,128)(2,1)S(1)}, u32[]{:S(2)}, u32[]{:S(2)}) collective-permute-start(bf16[448,128]{1,0:T(8,128)(2,1)} %get-tuple-element.31), channel_id=1, source_target_pairs={{0,240},{4,20},{8,248},{12,28},{16,0},{20,36},{24,8},{28,44},{32,1... | collective-permute-start | bytes 344072 | tf_op jit(solution)/shard_map/ppermute | solution.py:352
  12.6 10.4 %collective-permute-start.2 = (bf16[448,128]{1,0:T(8,128)(2,1)}, bf16[448,128]{1,0:T(8,128)(2,1)S(1)}, u32[]{:S(2)}, u32[]{:S(2)}) collective-permute-start(bf16[448,128]{1,0:T(8,128)(2,1)} %get-tuple-element.32), channel_id=1, source_target_pairs={{0,12},{4,248},{8,20},{12,0},{16,28},{20,8},{24,36},{28,16},{32,44... | collective-permute-start | bytes 344072 | tf_op jit(solution)/shard_map/ppermute | solution.py:352
  12.7 15.7 %collective-permute-start.3 = (bf16[448,128]{1,0:T(8,128)(2,1)}, bf16[448,128]{1,0:T(8,128)(2,1)S(1)}, u32[]{:S(2)}, u32[]{:S(2)}) collective-permute-start(bf16[448,128]{1,0:T(8,128)(2,1)} %get-tuple-element.33), channel_id=1, source_target_pairs={{0,244},{4,16},{8,252},{12,24},{16,4},{20,32},{24,12},{28,40},{32,... | collective-permute-start | bytes 344072 | tf_op jit(solution)/shard_map/ppermute | solution.py:352
  17.7 10.7 %collective-permute-start.4 = (bf16[448,128]{1,0:T(8,128)(2,1)}, bf16[448,128]{1,0:T(8,128)(2,1)S(1)}, u32[]{:S(2)}, u32[]{:S(2)}) collective-permute-start(bf16[448,128]{1,0:T(8,128)(2,1)} %get-tuple-element.34), channel_id=1, source_target_pairs={{0,8},{4,252},{8,16},{12,4},{16,24},{20,12},{24,32},{28,20},{32,40... | collective-permute-start | bytes 344072 | tf_op jit(solution)/shard_map/ppermute | solution.py:352
  18.7 9.7 %collective-permute-start.5 = (bf16[448,128]{1,0:T(8,128)(2,1)}, bf16[448,128]{1,0:T(8,128)(2,1)S(1)}, u32[]{:S(2)}, u32[]{:S(2)}) collective-permute-start(bf16[448,128]{1,0:T(8,128)(2,1)} %get-tuple-element.35), channel_id=1, source_target_pairs={{0,248},{4,12},{8,0},{12,20},{16,8},{20,28},{24,16},{28,36},{32,24... | collective-permute-start | bytes 344072 | tf_op jit(solution)/shard_map/ppermute | solution.py:352
  23.0 5.4 %collective-permute-start.6 = (bf16[448,128]{1,0:T(8,128)(2,1)}, bf16[448,128]{1,0:T(8,128)(2,1)S(1)}, u32[]{:S(2)}, u32[]{:S(2)}) collective-permute-start(bf16[448,128]{1,0:T(8,128)(2,1)} %get-tuple-element.36), channel_id=1, source_target_pairs={{0,4},{4,0},{8,12},{12,8},{16,20},{20,16},{24,28},{28,24},{32,36},... | collective-permute-start | bytes 344072 | tf_op jit(solution)/shard_map/ppermute | solution.py:352
  23.0 8.0 %collective-permute-start.7 = (bf16[448,128]{1,0:T(8,128)(2,1)}, bf16[448,128]{1,0:T(8,128)(2,1)S(1)}, u32[]{:S(2)}, u32[]{:S(2)}) collective-permute-start(bf16[448,128]{1,0:T(8,128)(2,1)} %get-tuple-element.37), channel_id=1, source_target_pairs={{0,252},{4,8},{8,4},{12,16},{16,12},{20,24},{24,20},{28,32},{32,28... | collective-permute-start | bytes 344072 | tf_op jit(solution)/shard_map/ppermute | solution.py:352
  24.7 1.0 %copy-start.1 = (bf16[1216,128]{1,0:T(8,128)(2,1)S(1)}, bf16[1216,128]{1,0:T(8,128)(2,1)}, u32[]{:S(2)}) copy-start(bf16[1216,128]{1,0:T(8,128)(2,1)} %get-tuple-element.22.own_in_ref) | copy-start | bytes 933892
  25.7 0.9 %copy-start.2 = (s32[96,256]{1,0:T(8,128)S(1)}, s32[96,256]{1,0:T(8,128)}, u32[]{:S(2)}) copy-start(s32[96,256]{1,0:T(8,128)} %get-tuple-element.23.ints_ref) | copy-start | bytes 294916
  59.2 4.3 %collective-permute-start.8 = (f32[64,256]{1,0:T(8,128)S(1)}, f32[64,256]{1,0:T(8,128)S(1)}, u32[]{:S(2)}, u32[]{:S(2)}) collective-permute-start(f32[64,256]{1,0:T(8,128)S(1)} %get-tuple-element.39), channel_id=1, source_target_pairs={{0,1},{1,2},{2,3},{3,0},{4,7},{5,4},{6,5},{7,6},{8,9},{9,10},{10,1... | collective-permute-start | bytes 196616 | tf_op jit(solution)/shard_map/ppermute | solution.py:363
  59.8 5.8 %collective-permute-start.9 = (f32[64,256]{1,0:T(8,128)S(1)}, f32[64,256]{1,0:T(8,128)S(1)}, u32[]{:S(2)}, u32[]{:S(2)}) collective-permute-start(f32[64,256]{1,0:T(8,128)S(1)} %get-tuple-element.40), channel_id=1, source_target_pairs={{0,2},{1,3},{2,0},{3,1},{4,6},{5,7},{6,4},{7,5},{8,10},{9,11},{10,... | collective-permute-start | bytes 196616 | tf_op jit(solution)/shard_map/ppermute | solution.py:363
  62.2 5.5 %collective-permute-start.10 = (f32[64,256]{1,0:T(8,128)S(1)}, f32[64,256]{1,0:T(8,128)S(1)}, u32[]{:S(2)}, u32[]{:S(2)}) collective-permute-start(f32[64,256]{1,0:T(8,128)S(1)} %get-tuple-element.41), channel_id=1, source_target_pairs={{0,3},{1,0},{2,1},{3,2},{4,5},{5,6},{6,7},{7,4},{8,11},{9,8},{10,9... | collective-permute-start | bytes 196616 | tf_op jit(solution)/shard_map/ppermute | solution.py:363

commit v5 on v4

--- a/solution.py
+++ b/solution.py
@@ -48,7 +48,8 @@
     reach = (PEERS - 1) // 2
     pairs = [(reach, reach)]
     for step in range(reach, 0, -1):
-        pairs += [(reach - step, reach + step), (reach + step, reach - step)]
+        pair = [(reach - step, reach + step), (reach + step, reach - step)]
+        pairs += pair[::-1] if step == 1 else pair
     return pairs
 
 
@@ -59,7 +60,7 @@
     step = abs(k - reach)
     first = 1 + 2 * (reach - step)
     upward = odd == step % 2
-    a, b = (first, first + 1) if k > reach else (first + 1, first)
+    a, b = (first, first + 1) if (k > reach) != (step == 1) else (first + 1, first)
     return jnp.where(upward, got[a][part], got[b][part])
 
 

time: 68 us -> 68.2 us (level)
  starting transfers between devices: 24 us -> 22.5 us
  waiting for transfers between devices: 8.11 us -> 9.29 us
    ppermute x8, starting transfers between devices: 21 us -> 19.6 us  [per_device(): got[i] = lax.ppermute(payload[i], 'slab', pairs)]
    ppermute x8, waiting for transfers between devices: 2.64 us -> 3.81 us  [per_device(): got[i] = lax.ppermute(payload[i], 'slab', pairs)]
  transfers between devices with their start and end apart: 11 -> 11, of which waited for: 4 -> 5; matrix products, arithmetic and copies ran while one was open for 0% -> 0% of each run, Pallas kernels for 3% -> 3%
where the time goes in v5:
time: 68.2 us; the launch traced here: 68 us
  Pallas kernels  33 us (48%)
  starting transfers between devices  22.5 us (33%)
  waiting for transfers between devices  9.29 us (14%)
  local copies, waits for them, and re-layouts  2.49 us (4%)
  between operations  0.73 us (1%)
    ppermute x8, starting transfers between devices, per_device(): got[i] = lax.ppermute(payload[i], 'slab', pairs)  19.6 us
    pallas_call x1, Pallas kernels, near(): pl.pallas_call(near_kernel, out_shape=jax.ShapeDtypeStruct((LEAVES, LANES...  16.1 us
    pallas_call x1, Pallas kernels, far(): pl.pallas_call(far_kernel, out_shape=[jax.ShapeDtypeStruct((LEAVES // 4,...  12 us
    ppermute x3, waiting for transfers between devices, per_device(): total = total + lax.ppermute(parts[step], ('slab', 'tile'), pairs)  5.47 us
    ppermute x8, waiting for transfers between devices, per_device(): got[i] = lax.ppermute(payload[i], 'slab', pairs)  3.81 us
    pallas_call x1, Pallas kernels, pack(): pl.pallas_call(pack_kernel, out_shape=[jax.ShapeDtypeStruct((PAYLOAD + 3...  3.04 us
    ppermute x3, starting transfers between devices, per_device(): total = total + lax.ppermute(parts[step], ('slab', 'tile'), pairs)  2.95 us
    unnamed x6, local copies, waits for them, and re-layouts  1.86 us
  transfers between devices with their start and end apart: 11, of which 5 were waited for; matrix products, arithmetic and copies ran while one was open for 0% of the time, Pallas kernels for 3%

profile of v5, /device:TPU:6, one launch (start us, length us, event | category | flops | bytes accessed | tf_op | source)
XLA Modules:
  0.0 68.0 jit_solution(14940304322700389675)
XLA Ops:
  0.6 0.0 copy-start
  0.6 3.0 %pack.1 = (bf16[1216,128]{1,0:T(8,128)(2,1)}, bf16[448,128]{1,0:T(8,128)(2,1)}, bf16[448,128]{1,0:T(8,128)(2,1)}, bf16[448,128]{1,0:T(8,128)(2,1)}, bf16[448,128...) custom-call(s32[1]{0:T(128)} %bitcast.1.odd_ref, ...), custom_call_target="tpu_custom_call" | custom-call | tf_op jit(solution)/shard_map/pack/pallas_call | solution.py:98
  3.7 3.3 %collective-permute-start = (bf16[448,128]{1,0:T(8,128)(2,1)}, bf16[448,128]{1,0:T(8,128)(2,1)S(1)}, u32[]{:S(2)}, u32[]{:S(2)}) collective-permute-start(bf16[448,128]{1,0:T(8,128)(2,1)} %get-tuple-element.30), channel_id=1, source_target_pairs={{0,16},{4,244},{8,24},{12,252},{16,32},{20,4},{24,40},{28,12},{32,... | collective-permute-start | bytes 344072 | tf_op jit(solution)/shard_map/ppermute | solution.py:353
  7.1 5.6 %collective-permute-start.1 = (bf16[448,128]{1,0:T(8,128)(2,1)}, bf16[448,128]{1,0:T(8,128)(2,1)S(1)}, u32[]{:S(2)}, u32[]{:S(2)}) collective-permute-start(bf16[448,128]{1,0:T(8,128)(2,1)} %get-tuple-element.31), channel_id=1, source_target_pairs={{0,240},{4,20},{8,248},{12,28},{16,0},{20,36},{24,8},{28,44},{32,1... | collective-permute-start | bytes 344072 | tf_op jit(solution)/shard_map/ppermute | solution.py:353
  12.6 0.1 collective-permute-start.2
  12.7 4.9 %collective-permute-start.3 = (bf16[448,128]{1,0:T(8,128)(2,1)}, bf16[448,128]{1,0:T(8,128)(2,1)S(1)}, u32[]{:S(2)}, u32[]{:S(2)}) collective-permute-start(bf16[448,128]{1,0:T(8,128)(2,1)} %get-tuple-element.33), channel_id=1, source_target_pairs={{0,244},{4,16},{8,252},{12,24},{16,4},{20,32},{24,12},{28,40},{32,... | collective-permute-start | bytes 344072 | tf_op jit(solution)/shard_map/ppermute | solution.py:353
  17.7 1.0 %collective-permute-start.4 = (bf16[448,128]{1,0:T(8,128)(2,1)}, bf16[448,128]{1,0:T(8,128)(2,1)S(1)}, u32[]{:S(2)}, u32[]{:S(2)}) collective-permute-start(bf16[448,128]{1,0:T(8,128)(2,1)} %get-tuple-element.34), channel_id=1, source_target_pairs={{0,8},{4,252},{8,16},{12,4},{16,24},{20,12},{24,32},{28,20},{32,40... | collective-permute-start | bytes 344072 | tf_op jit(solution)/shard_map/ppermute | solution.py:353
  18.7 0.0 collective-permute-done.refs_1_
  18.7 4.3 %collective-permute-start.5 = (bf16[448,128]{1,0:T(8,128)(2,1)}, bf16[448,128]{1,0:T(8,128)(2,1)S(1)}, u32[]{:S(2)}, u32[]{:S(2)}) collective-permute-start(bf16[448,128]{1,0:T(8,128)(2,1)} %get-tuple-element.35), channel_id=1, source_target_pairs={{0,248},{4,12},{8,0},{12,20},{16,8},{20,28},{24,16},{28,36},{32,24... | collective-permute-start | bytes 344072 | tf_op jit(solution)/shard_map/ppermute | solution.py:353
  23.0 0.0 collective-permute-done.1.refs_2_
  23.0 0.0 collective-permute-start.6
  23.0 0.0 collective-permute-done.2.refs_3_
  23.0 0.3 collective-permute-start.7
  23.3 0.0 copy-start.1
  23.3 1.0 %copy-done.1 = bf16[1216,128]{1,0:T(8,128)(2,1)S(1)} copy-done((bf16[1216,128]{1,0:T(8,128)(2,1)S(1)}, bf16[1216,128]{1,0:T(8,128)(2,1)}, u32[]{:S(2)}) %copy-start.1) | copy-done | bytes 311320
  24.3 0.0 copy-start.2
  24.3 0.9 %copy-done.2 = s32[96,256]{1,0:T(8,128)S(1)} copy-done((s32[96,256]{1,0:T(8,128)S(1)}, s32[96,256]{1,0:T(8,128)}, u32[]{:S(2)}) %copy-start.2) | copy-done | bytes 98328
  25.2 1.8 %prep.1 = (bf16[32,128,128]{2,1,0:T(8,128)(2,1)S(1)}, s32[8,256]{1,0:T(8,128)S(1)}, f32[256,128]{1,0:T(8,128)S(1)}, s32[16]{0:T(128)S(1)}, s32[8,256]{1,0:T(8,128)S(1)}, /*index=5*/bf16[448,128]{1,0:T(8,128)(2,1)S(1)}) custom-call(bf16[1216,128]{1,0:T(8,128)(2,1)S(1)} %copy-done.1, s32[96,256]{1,0:T(8,128)S(1)} %copy-done.2), custom_call_target="tpu_custom_call" | custom-call | tf_op jit(solution)/shard_map/prep/pallas_call | solution.py:179
  27.0 0.0 collective-permute-done.3.refs_4_
  27.0 0.3 collective-permute-done.4.refs_5_
  27.3 0.0 collective-permute-done.5.refs_6_
  27.3 3.5 %collective-permute-done.6.refs_7_ = bf16[448,128]{1,0:T(8,128)(2,1)S(1)} collective-permute-done((bf16[448,128]{1,0:T(8,128)(2,1)}, bf16[448,128]{1,0:T(8,128)(2,1)S(1)}, u32[]{:S(2)}, u32[]{:S(2)}) %collective-permute-start.6) | collective-permute-done | bytes 114720 | tf_op jit(solution)/shard_map/ppermute | solution.py:353
  30.8 0.0 collective-permute-done.7.refs_8_
  30.8 16.1 %near.1.near_ref = f32[256,128]{1,0:T(8,128)S(1)} custom-call(s32[1]{0:T(128)} %bitcast.1.odd_ref, s32[8,256]{1,0:T(8,128)S(1)} %get-tuple-element.26.order, s32[8,256]{1,0:T(8,128)S(1)} %get-tuple-element.27.slot, bf16[32,128,128]{2,1,0:T(8,128)(2,1)S(1)} %get-tuple-element.28.lhs_ref, bf16[448,128]{1,0:T(8,128)(2,1)S(1)} %get-tuple-element.29.refs_0_, ...), custom_call_target="tpu_custom_call" | custom-call | tf_op jit(solution)/shard_map/near/pallas_call | solution.py:252
  46.9 0.0 copy-done
  46.9 12.0 %far.1 = (f32[64,256]{1,0:T(8,128)S(1)}, f32[64,256]{1,0:T(8,128)S(1)}, f32[64,256]{1,0:T(8,128)S(1)}, f32[64,256]{1,0:T(8,128)S(1)}) custom-call(s32[1]{0:T(128)} %bitcast.tile_ref, s32[1]{0:T(128)} %bitcast.1.odd_ref, s32[16]{0:T(128)S(1)} %get-tuple-element.24.base_ref, f32[256,128]{1,0:T(8,128)S(1)} %get-tuple-element.25.code_ref, ...), custom_call_target="tpu_custom_call" | custom-call | tf_op jit(solution)/shard_map/far/pallas_call | solution.py:324
  59.0 0.5 collective-permute-start.8
  59.5 2.4 %collective-permute-start.9 = (f32[64,256]{1,0:T(8,128)S(1)}, f32[64,256]{1,0:T(8,128)S(1)}, u32[]{:S(2)}, u32[]{:S(2)}) collective-permute-start(f32[64,256]{1,0:T(8,128)S(1)} %get-tuple-element.40), channel_id=1, source_target_pairs={{0,2},{1,3},{2,0},{3,1},{4,6},{5,7},{6,4},{7,5},{8,10},{9,11},{10,... | collective-permute-start | bytes 196616 | tf_op jit(solution)/shard_map/ppermute | solution.py:364
  61.9 0.0 collective-permute-start.10
  61.9 1.4 %collective-permute-done.8 = f32[64,256]{1,0:T(8,128)S(1)} collective-permute-done((f32[64,256]{1,0:T(8,128)S(1)}, f32[64,256]{1,0:T(8,128)S(1)}, u32[]{:S(2)}, u32[]{:S(2)}) %collective-permute-start.8) | collective-permute-done | bytes 65568 | tf_op jit(solution)/shard_map/ppermute | solution.py:364
  63.3 1.9 %collective-permute-done.9 = f32[64,256]{1,0:T(8,128)S(1)} collective-permute-done((f32[64,256]{1,0:T(8,128)S(1)}, f32[64,256]{1,0:T(8,128)S(1)}, u32[]{:S(2)}, u32[]{:S(2)}) %collective-permute-start.9) | collective-permute-done | bytes 65568 | tf_op jit(solution)/shard_map/ppermute | solution.py:364
  65.2 2.1 %collective-permute-done.10 = f32[64,256]{1,0:T(8,128)S(1)} collective-permute-done((f32[64,256]{1,0:T(8,128)S(1)}, f32[64,256]{1,0:T(8,128)S(1)}, u32[]{:S(2)}, u32[]{:S(2)}) %collective-permute-start.10) | collective-permute-done | bytes 65568 | tf_op jit(solution)/shard_map/ppermute | solution.py:364
  67.4 0.6 fusion
  (1 shorter events, 0.0 us)
Async XLA Ops:
  0.6 46.3 %copy-start = (bf16[79,128,128]{2,1,0:T(8,128)(2,1)S(1)}, bf16[79,128,128]{2,1,0:T(8,128)(2,1)}, u32[]{:S(2)}) copy-start(bf16[79,128,128]{2,1,0:T(8,128)(2,1)} %m2l_h.1) | copy-start | bytes 7766020
  3.7 15.0 %collective-permute-start = (bf16[448,128]{1,0:T(8,128)(2,1)}, bf16[448,128]{1,0:T(8,128)(2,1)S(1)}, u32[]{:S(2)}, u32[]{:S(2)}) collective-permute-start(bf16[448,128]{1,0:T(8,128)(2,1)} %get-tuple-element.30), channel_id=1, source_target_pairs={{0,16},{4,244},{8,24},{12,252},{16,32},{20,4},{24,40},{28,12},{32,... | collective-permute-start | bytes 344072 | tf_op jit(solution)/shard_map/ppermute | solution.py:353
  7.1 16.0 %collective-permute-start.1 = (bf16[448,128]{1,0:T(8,128)(2,1)}, bf16[448,128]{1,0:T(8,128)(2,1)S(1)}, u32[]{:S(2)}, u32[]{:S(2)}) collective-permute-start(bf16[448,128]{1,0:T(8,128)(2,1)} %get-tuple-element.31), channel_id=1, source_target_pairs={{0,240},{4,20},{8,248},{12,28},{16,0},{20,36},{24,8},{28,44},{32,1... | collective-permute-start | bytes 344072 | tf_op jit(solution)/shard_map/ppermute | solution.py:353
  12.6 10.4 %collective-permute-start.2 = (bf16[448,128]{1,0:T(8,128)(2,1)}, bf16[448,128]{1,0:T(8,128)(2,1)S(1)}, u32[]{:S(2)}, u32[]{:S(2)}) collective-permute-start(bf16[448,128]{1,0:T(8,128)(2,1)} %get-tuple-element.32), channel_id=1, source_target_pairs={{0,12},{4,248},{8,20},{12,0},{16,28},{20,8},{24,36},{28,16},{32,44... | collective-permute-start | bytes 344072 | tf_op jit(solution)/shard_map/ppermute | solution.py:353
  12.7 14.2 %collective-permute-start.3 = (bf16[448,128]{1,0:T(8,128)(2,1)}, bf16[448,128]{1,0:T(8,128)(2,1)S(1)}, u32[]{:S(2)}, u32[]{:S(2)}) collective-permute-start(bf16[448,128]{1,0:T(8,128)(2,1)} %get-tuple-element.33), channel_id=1, source_target_pairs={{0,244},{4,16},{8,252},{12,24},{16,4},{20,32},{24,12},{28,40},{32,... | collective-permute-start | bytes 344072 | tf_op jit(solution)/shard_map/ppermute | solution.py:353
  17.7 9.6 %collective-permute-start.4 = (bf16[448,128]{1,0:T(8,128)(2,1)}, bf16[448,128]{1,0:T(8,128)(2,1)S(1)}, u32[]{:S(2)}, u32[]{:S(2)}) collective-permute-start(bf16[448,128]{1,0:T(8,128)(2,1)} %get-tuple-element.34), channel_id=1, source_target_pairs={{0,8},{4,252},{8,16},{12,4},{16,24},{20,12},{24,32},{28,20},{32,40... | collective-permute-start | bytes 344072 | tf_op jit(solution)/shard_map/ppermute | solution.py:353
  18.7 8.6 %collective-permute-start.5 = (bf16[448,128]{1,0:T(8,128)(2,1)}, bf16[448,128]{1,0:T(8,128)(2,1)S(1)}, u32[]{:S(2)}, u32[]{:S(2)}) collective-permute-start(bf16[448,128]{1,0:T(8,128)(2,1)} %get-tuple-element.35), channel_id=1, source_target_pairs={{0,248},{4,12},{8,0},{12,20},{16,8},{20,28},{24,16},{28,36},{32,24... | collective-permute-start | bytes 344072 | tf_op jit(solution)/shard_map/ppermute | solution.py:353
  23.0 7.7 %collective-permute-start.6 = (bf16[448,128]{1,0:T(8,128)(2,1)}, bf16[448,128]{1,0:T(8,128)(2,1)S(1)}, u32[]{:S(2)}, u32[]{:S(2)}) collective-permute-start(bf16[448,128]{1,0:T(8,128)(2,1)} %get-tuple-element.36), channel_id=1, source_target_pairs={{0,252},{4,8},{8,4},{12,16},{16,12},{20,24},{24,20},{28,32},{32,28... | collective-permute-start | bytes 344072 | tf_op jit(solution)/shard_map/ppermute | solution.py:353
  23.0 7.7 %collective-permute-start.7 = (bf16[448,128]{1,0:T(8,128)(2,1)}, bf16[448,128]{1,0:T(8,128)(2,1)S(1)}, u32[]{:S(2)}, u32[]{:S(2)}) collective-permute-start(bf16[448,128]{1,0:T(8,128)(2,1)} %get-tuple-element.37), channel_id=1, source_target_pairs={{0,4},{4,0},{8,12},{12,8},{16,20},{20,16},{24,28},{28,24},{32,36},... | collective-permute-start | bytes 344072 | tf_op jit(solution)/shard_map/ppermute | solution.py:353
  23.3 1.0 %copy-start.1 = (bf16[1216,128]{1,0:T(8,128)(2,1)S(1)}, bf16[1216,128]{1,0:T(8,128)(2,1)}, u32[]{:S(2)}) copy-start(bf16[1216,128]{1,0:T(8,128)(2,1)} %get-tuple-element.22.own_in_ref) | copy-start | bytes 933892
  24.3 0.9 %copy-start.2 = (s32[96,256]{1,0:T(8,128)S(1)}, s32[96,256]{1,0:T(8,128)}, u32[]{:S(2)}) copy-start(s32[96,256]{1,0:T(8,128)} %get-tuple-element.23.ints_ref) | copy-start | bytes 294916
  59.0 4.3 %collective-permute-start.8 = (f32[64,256]{1,0:T(8,128)S(1)}, f32[64,256]{1,0:T(8,128)S(1)}, u32[]{:S(2)}, u32[]{:S(2)}) collective-permute-start(f32[64,256]{1,0:T(8,128)S(1)} %get-tuple-element.39), channel_id=1, source_target_pairs={{0,1},{1,2},{2,3},{3,0},{4,7},{5,4},{6,5},{7,6},{8,9},{9,10},{10,1... | collective-permute-start | bytes 196616 | tf_op jit(solution)/shard_map/ppermute | solution.py:364
  59.5 5.8 %collective-permute-start.9 = (f32[64,256]{1,0:T(8,128)S(1)}, f32[64,256]{1,0:T(8,128)S(1)}, u32[]{:S(2)}, u32[]{:S(2)}) collective-permute-start(f32[64,256]{1,0:T(8,128)S(1)} %get-tuple-element.40), channel_id=1, source_target_pairs={{0,2},{1,3},{2,0},{3,1},{4,6},{5,7},{6,4},{7,5},{8,10},{9,11},{10,... | collective-permute-start | bytes 196616 | tf_op jit(solution)/shard_map/ppermute | solution.py:364
  61.9 5.5 %collective-permute-start.10 = (f32[64,256]{1,0:T(8,128)S(1)}, f32[64,256]{1,0:T(8,128)S(1)}, u32[]{:S(2)}, u32[]{:S(2)}) collective-permute-start(f32[64,256]{1,0:T(8,128)S(1)} %get-tuple-element.41), channel_id=1, source_target_pairs={{0,3},{1,0},{2,1},{3,2},{4,5},{5,6},{6,7},{7,4},{8,11},{9,8},{10,9... | collective-permute-start | bytes 196616 | tf_op jit(solution)/shard_map/ppermute | solution.py:364
